TPU v7x, 256 devices: a whole 4x4x8 slice. The times are simulated.
256 devices in a mesh: section: 4 (over x), dp: 64 (over y, z, core).
Axes of the slice: x: 4, y: 4, z: 8, core: 2. Of those that a mesh axis runs over, the one named last changes fastest.
Arguments:
- acts: bfloat16 [4, 8192, 4096], P('section', 'dp'), may hold values from -6 to 6
- grad_rows: bfloat16 [4, 8192, 8192], P('section', 'dp'), may hold values from -6 to 6
- block_experts: int32 [4, 64, 2], P('section'), may hold values from 0 to 7, all different within a row
Outputs:
- weight_grad: bfloat16 [4, 64, 512, 1024], P('section', 'dp')
All inputs are finite; a program needn't handle non-finite values.
Results may differ from a plain program's by a relative error of at most 0.001.
Values may be sent and summed in bfloat16 or wider, within the bound.
No kernel may reach another device: no remote copies, remote signals or barrier semaphores. Data moves between devices by JAX's collectives and lax.ppermute only.
A program may use at most 128 MiB of HBM per device.

v0:
```python
import math

import jax
import jax.numpy as jnp
from jax import lax
from jax.experimental import pallas as pl
from jax.experimental.pallas import tpu as pltpu
from jax.sharding import Mesh
from jax.sharding import PartitionSpec as P

DW = 4096
HW = 8192
BLOCK = 128
DGRID = 8
HGRID = 8
BLOCKS = 64
SUB = BLOCK // DGRID
TR = DW // DGRID
TC = HW // HGRID
NY = 4
NX = 4

NZ = 8
MTILE = 256

MAIN = 20
MORE = 28
DP = ("y", "zh", "zl", "core")


def pack_kernel(acts_ref, grads_ref, out_ref):
    for a in range(2):
        for c in range(HGRID):
            out_ref[a * HGRID + c, :, :TR] = acts_ref[c * SUB:(c + 1) * SUB, a * TR:(a + 1) * TR]
            out_ref[a * HGRID + c, :, TR:] = grads_ref[a * SUB:(a + 1) * SUB, c * TC:(c + 1) * TC]


def pack(acts, grads):
    return pl.pallas_call(
        pack_kernel,
        grid=(DGRID // 2,),
        in_specs=[
            pl.BlockSpec((BLOCK, 2 * TR), lambda a: (0, a)),
            pl.BlockSpec((2 * SUB, HW), lambda a: (a, 0)),
        ],
        out_specs=pl.BlockSpec((2 * HGRID, SUB, TR + TC), lambda a: (a, 0, 0)),
        out_shape=jax.ShapeDtypeStruct((DGRID * HGRID, SUB, TR + TC), jnp.bfloat16),
    )(acts, grads)


def compact_kernel(cap, aidx, gidx, count, recv, acts_out, grads_out, asem, gsem):
    def acopy(k):
        return pltpu.make_async_copy(recv.at[aidx[k], :, pl.ds(0, TR)], acts_out.at[k], asem.at[k])

    def gcopy(k):
        return pltpu.make_async_copy(recv.at[gidx[k], :, pl.ds(TR, TC)], grads_out.at[k], gsem.at[k])

    def start(k, carry):
        gcopy(k).start()
        acopy(k).start()
        return carry

    def finish(k, carry):
        gcopy(k).wait()
        acopy(k).wait()
        return carry

    lax.fori_loop(0, cap, start, 0)
    lax.fori_loop(0, cap, finish, 0)

    def clear(k, carry):
        acts_out[k] = jnp.zeros((SUB, TR), jnp.bfloat16)
        return carry

    lax.fori_loop(count[0], cap, clear, 0)


def compact(cap, recv, aidx, gidx, count):
    smem = pl.BlockSpec(memory_space=pltpu.SMEM)
    vmem = pl.BlockSpec(memory_space=pltpu.VMEM)
    return pl.pallas_call(
        lambda *refs: compact_kernel(cap, *refs),
        in_specs=[smem, smem, smem, pl.BlockSpec(memory_space=pl.ANY)],
        out_specs=[vmem, vmem],
        out_shape=[
            jax.ShapeDtypeStruct((cap, SUB, TR), jnp.bfloat16),
            jax.ShapeDtypeStruct((cap, SUB, TC), jnp.bfloat16),
        ],
        scratch_shapes=[pltpu.SemaphoreType.DMA((cap,)), pltpu.SemaphoreType.DMA((cap,))],
    )(aidx, gidx, count, recv)


def order_of(touched):
    blocks = jnp.arange(BLOCKS)
    rank = jnp.sum((blocks[None, :] < blocks[:, None]) & touched[None, :], axis=1)
    hit = touched[None, :] & (rank[None, :] == blocks[:, None])
    return jnp.sum(jnp.where(hit, blocks[None, :], 0), axis=1).astype(jnp.int32)


def ring(axis, size, distance):
    return [(i, (i + distance) % size) for i in range(size)]


def product_kernel(n, scale, has_total, *refs):
    where, acts = refs[0], refs[1]
    pieces, rest = refs[2:2 + n], refs[2 + n:]
    out = rest[-1]

    def tile(t, carry):
        rows = pl.ds(pl.multiple_of(t * MTILE, MTILE), MTILE)
        total = rest[0][rows, :] if has_total else None
        for i in range(n):
            now = lax.dot_general(
                acts[where[i], :, rows], pieces[i][...],
                (((0,), (0,)), ((), ())), preferred_element_type=jnp.float32,
            )
            total = now if total is None else total + now
        out[rows, :] = (total * scale).astype(out.dtype)
        return carry

    lax.fori_loop(0, TR // MTILE, tile, 0)


def products(where, acts, pieces, total, dtype, scale=1.0):
    rows = acts.shape[1]
    vmem = pl.BlockSpec(memory_space=pltpu.VMEM)
    arrays = [acts] + [p.reshape(rows, TC) for p in pieces] + ([] if total is None else [total])
    return pl.pallas_call(
        lambda *refs: product_kernel(len(pieces), scale, total is not None, *refs),
        in_specs=[pl.BlockSpec(memory_space=pltpu.SMEM)] + [vmem] * len(arrays),
        out_specs=vmem,
        out_shape=jax.ShapeDtypeStruct((TR, TC), dtype),
        cost_estimate=pl.CostEstimate(
            flops=2 * len(pieces) * rows * TR * TC,
            bytes_accessed=len(pieces) * rows * (TR + TC) * 2 + 4 * TR * TC, transcendentals=0,
        ),
        compiler_params=pltpu.CompilerParams(vmem_limit_bytes=40 << 20),
    )(where, *arrays)


def gather_and_multiply(cap, recv, aidx, gidx, count, total, dtype, scale):
    y, zh, core = lax.axis_index("y"), lax.axis_index("zh"), lax.axis_index("core")
    acts_c, grads_c = compact(cap, recv, aidx, gidx, count)
    near = lax.ppermute(grads_c, "x", ring("x", NX, -1))
    plane = [(z, c) for z in range(NZ) for c in range(2)]
    hop = [((z * 2 + c), (z + (2 if c == 0 else -2)) % NZ * 2 + c) for z, c in plane]
    far = lax.ppermute(grads_c, ("zh", "zl", "core"), hop)
    far, near, acts_c = lax.optimization_barrier((far, near, acts_c))
    far = lax.ppermute(
        far, ("x", "zh", "zl", "core"),
        [(s * 2 * NZ + i, (s - 1) % NX * 2 * NZ + j) for s in range(NX) for i, j in hop],
    )
    acts_all = lax.all_gather(acts_c, ("zl", "core")).reshape(DGRID, cap * SUB, TR)

    def beside(own):
        up = lax.ppermute(own, "y", ring("y", NY, 1))
        down = lax.ppermute(own, "y", ring("y", NY, -1))
        return up, down

    def across(up, down):
        way = [(yy * 2 + c, (yy + (1 if c == 0 else -1)) % NY * 2 + c) for yy in range(NY) for c in range(2)]
        pairs = [(i // 2 * 2 * NZ + i % 2, j // 2 * 2 * NZ + j % 2) for i, j in way]
        pairs = [(i + 2 * z, j + 2 * z) for z in range(NZ) for i, j in pairs]
        return lax.ppermute(jnp.where(core == 0, up, down), DP, pairs)

    def places(flip):
        h = 1 - zh if flip else zh
        return jnp.stack([lax.rem(y + NY - d, NY) * 2 + h for d in (0, 1, 3, 2)]).astype(jnp.int32)

    up, down = beside(near)
    third = across(up, down)
    far_up, far_down = beside(far)
    far_third = across(far_up, far_down)
    here, there = places(False), places(True)
    total = products(here[:3], acts_all, (near, up, down), total, jnp.float32)
    both = jnp.concatenate([here[3:], there[:3]])
    total = products(both, acts_all, (third, far, far_up, far_down), total, jnp.float32)
    return products(there[3:], acts_all, (far_third,), total, dtype, scale)


def shards(acts, grad_rows, block_experts):
    packed = pack(acts[0], grad_rows[0])
    behind = [block_experts] + [
        lax.ppermute(block_experts, "x", ring("x", NX, d)) for d in (1, 2, 3)
    ]
    touched = [jnp.any(b[0] == 0, axis=1) for b in behind]
    counts = [jnp.sum(t.astype(jnp.int32)) for t in touched]
    most = jnp.maximum(jnp.maximum(counts[0], counts[1]), jnp.maximum(counts[2], counts[3]))
    aidx, gidx = order_of(touched[0]), order_of(touched[1])
    recv = lax.all_to_all(packed, DP, split_axis=0, concat_axis=0, tiled=True)

    scale = 2.0 / math.sqrt(BLOCKS * BLOCK)

    def straight(cap):
        def run(recv, aidx, gidx, count, most):
            return gather_and_multiply(
                cap, recv, aidx[:cap], gidx[:cap], jnp.minimum(count, cap), None, jnp.bfloat16, scale
            )
        return run

    def rounds(recv, aidx, gidx, count, most):
        def one(j, total):
            start = j * MORE
            return gather_and_multiply(
                MORE, recv,
                lax.dynamic_slice_in_dim(aidx, start, MORE),
                lax.dynamic_slice_in_dim(gidx, start, MORE),
                jnp.clip(count - start, 0, MORE), total, jnp.float32, 1.0,
            )

        turns = (most + MORE - 1) // MORE
        total = lax.fori_loop(0, turns, one, jnp.zeros((TR, TC), jnp.float32))
        return (total * scale).astype(jnp.bfloat16)

    out = lax.switch(
        (most > MAIN).astype(jnp.int32), [straight(MAIN), rounds],
        recv, aidx, gidx, counts[0].reshape(1), most,
    )
    return out[None, None]


def solution(mesh):
    fine = Mesh(mesh.devices.reshape(NX, NY, 2, 4, 2), ("x",) + DP)
    return jax.shard_map(
        shards,
        mesh=fine,
        in_specs=(P("x", DP, None), P("x", DP, None), P("x", None, None)),
        out_specs=P("x", DP, None, None),
        check_vma=False,
    )
```

profile of v0, /device:TPU:6, one launch (start us, length us, event | category | flops | bytes accessed | tf_op | source)
XLA Modules:
  0.0 191.3 jit_solution(15189306428356562117)
XLA Ops:
  6.5 4.2 %shard_map.39 = bf16[64,16,1536]{2,1,0:T(8,128)(2,1)} custom-call(bf16[128,4096]{1,0:T(8,128)(2,1)} %bitcast.95, bf16[128,8192]{1,0:T(8,128)(2,1)} %bitcast.93), custom_call_target="tpu_custom_call" | custom-call | tf_op jit(solution)/shard_map/pallas_call | solution.py:39
  10.7 0.0 copy-start.7
  10.7 12.2 %all-to-all-start = ((bf16[64,16,1536]{2,1,0:T(8,128)(2,1)}), bf16[64,16,1536]{2,1,0:T(8,128)(2,1)S(1)}, u32[]{:S(2)}, u32[]{:S(2)}) async-start(bf16[64,16,1536]{2,1,0:T(8,128)(2,1)} %shard_map.39), calls=%async_computation | async-start | bytes 6291456 | tf_op jit(solution)/shard_map/all_to_all | solution.py:190
  23.0 0.0 copy-done.7
  23.0 0.6 collective-permute-start.18
  23.5 1.5 collective-permute-start.20
  25.1 1.4 collective-permute-start.19
  26.5 0.1 convert_reduce_fusion.1
  26.6 0.1 select_reduce_fusion.1
  26.7 0.7 convert_reduce_fusion.5
  27.4 0.0 collective-permute-done.18
  27.5 0.6 convert_reduce_fusion.4
  28.1 0.2 collective-permute-done.20
  29.6 0.5 collective-permute-done.19
  30.2 0.6 convert_reduce_fusion.2
  30.8 0.6 convert_reduce_fusion.3
  32.7 0.1 convert_reduce_fusion
  32.8 0.1 select_reduce_fusion
  32.9 63.4 %all-to-all-done = bf16[64,16,1536]{2,1,0:T(8,128)(2,1)S(1)} async-done(((bf16[64,16,1536]{2,1,0:T(8,128)(2,1)}), bf16[64,16,1536]{2,1,0:T(8,128)(2,1)S(1)}, u32[]{:S(2)}, u32[]{:S(2)}) %all-to-all-start) | async-done | bytes 3145760 | tf_op jit(solution)/shard_map/all_to_all | solution.py:190
  96.3 87.2 %conditional.1 = (bf16[1,1,512,1024]{3,2,1,0:T(8,128)(2,1)S(1)}) conditional(s32[]{:T(128)} %clamp.3, (s32[64]{0:T(128)S(1)}, s32[64]{0:T(128)S(1)}, s32[1]{0:T(128)}, bf16[64,16,1536]{2,1,0:T(8,128)(2,1)S(1)}) %tuple.35, (s32[]{:T(128)}, s32[64]{0:T(128)S(1)}, s32[64]{0:T(128)S(1)}, s32[1]{0:T(128)}, bf16[64,16,1536]{2,1,0:T(8,128)(2,1)S(1)}) %tuple.36), branch_computations={%region_12.13_spmd, %region_13.16_spmd} | conditional | flops 3760062464 | bytes 127993888 | solution.py:215
  96.3 0.0 all-gather.7.cloned.1.call-start
  96.9 3.0 %branch_0_fun.4 = (bf16[20,16,512]{2,1,0:T(8,128)(2,1)}, bf16[20,16,1024]{2,1,0:T(8,128)(2,1)}) custom-call(s32[20]{0:T(128)S(1)} %bitcast.96, s32[20]{0:T(128)S(1)} %bitcast.97, s32[1]{0:T(128)S(6)} %min.8.refs_2_, bf16[64,16,1536]{2,1,0:T(8,128)(2,1)S(1)} %get-tuple-element.167.refs_3_), custom_call_target="tpu_custom_call" | custom-call | tf_op jit(solution)/shard_map/cond/branch_0_fun/pallas_call | solution.py:81
  99.9 1.3 collective-permute-start
  101.2 0.8 collective-permute-start.1
  102.0 16.3 %collective-permute-done = bf16[20,16,1024]{2,1,0:T(8,128)(2,1)S(1)} collective-permute-done((bf16[20,16,1024]{2,1,0:T(8,128)(2,1)}, bf16[20,16,1024]{2,1,0:T(8,128)(2,1)S(1)}, u32[]{:S(2)}, u32[]{:S(2)}) %collective-permute-start) | collective-permute-done | bytes 655392 | tf_op jit(solution)/shard_map/cond/branch_0_fun/ppermute | solution.py:147
  118.3 1.2 collective-permute-done.1
  119.6 0.0 all-gather.7.cloned.1.call-update
  119.6 0.6 collective-permute-start.2
  120.1 1.2 collective-permute-start.6
  121.4 2.0 %collective-permute-start.7 = (bf16[20,16,1024]{2,1,0:T(8,128)(2,1)}, bf16[20,16,1024]{2,1,0:T(8,128)(2,1)S(1)}, u32[]{:S(2)}, u32[]{:S(2)}) collective-permute-start(bf16[20,16,1024]{2,1,0:T(8,128)(2,1)} %collective-permute-done.1), channel_id=1, source_target_pairs={{0,48},{16,0},{32,16},{48,32},{1,49},{17,1},{33,17},{49,33},{2,50}... | collective-permute-start | bytes 1966088 | tf_op jit(solution)/shard_map/cond/branch_0_fun/ppermute | solution.py:157
  123.4 21.7 %collective-permute-done.2 = bf16[20,16,1024]{2,1,0:T(8,128)(2,1)S(1)} collective-permute-done((bf16[20,16,1024]{2,1,0:T(8,128)(2,1)S(1)}, bf16[20,16,1024]{2,1,0:T(8,128)(2,1)S(1)}, u32[]{:S(2)}, u32[]{:S(2)}) %collective-permute-start.2) | collective-permute-done | bytes 655392 | tf_op jit(solution)/shard_map/cond/branch_0_fun/ppermute | solution.py:149
  145.0 3.3 %collective-permute-start.4 = (bf16[20,16,1024]{2,1,0:T(8,128)(2,1)S(1)}, bf16[20,16,1024]{2,1,0:T(8,128)(2,1)S(1)}, u32[]{:S(2)}, u32[]{:S(2)}) collective-permute-start(bf16[20,16,1024]{2,1,0:T(8,128)(2,1)S(1)} %collective-permute-done.2), channel_id=1, source_target_pairs={{0,48},{16,0},{32,16},{48,32},{1,49},{17,1},{33,17},{49,33},{2,50}... | collective-permute-start | bytes 1966088 | tf_op jit(solution)/shard_map/cond/branch_0_fun/ppermute | solution.py:157
  148.3 3.6 %collective-permute-start.3 = (bf16[20,16,1024]{2,1,0:T(8,128)(2,1)S(1)}, bf16[20,16,1024]{2,1,0:T(8,128)(2,1)S(1)}, u32[]{:S(2)}, u32[]{:S(2)}) collective-permute-start(bf16[20,16,1024]{2,1,0:T(8,128)(2,1)S(1)} %collective-permute-done.2), channel_id=1, source_target_pairs={{0,16},{16,32},{32,48},{48,0},{1,17},{17,33},{33,49},{49,1},{2,18}... | collective-permute-start | bytes 1966088 | tf_op jit(solution)/shard_map/cond/branch_0_fun/ppermute | solution.py:156
  151.9 0.0 collective-permute-done.6
  151.9 0.0 collective-permute-done.7
  151.9 0.9 broadcast_select_fusion
  152.8 2.0 %collective-permute-start.8 = (bf16[20,16,1024]{2,1,0:T(8,128)(2,1)}, bf16[20,16,1024]{2,1,0:T(8,128)(2,1)}, u32[]{:S(2)}, u32[]{:S(2)}) collective-permute-start(bf16[20,16,1024]{2,1,0:T(8,128)(2,1)} %broadcast_select_fusion), channel_id=1, source_target_pairs={{0,16},{1,49},{16,32},{17,1},{32,48},{33,17},{48,0},{49,33},{2,18}... | collective-permute-start | bytes 1966088 | tf_op jit(solution)/shard_map/cond/branch_0_fun/ppermute | solution.py:164
  154.8 12.7 %collective-permute-done.4 = bf16[20,16,1024]{2,1,0:T(8,128)(2,1)S(1)} collective-permute-done((bf16[20,16,1024]{2,1,0:T(8,128)(2,1)S(1)}, bf16[20,16,1024]{2,1,0:T(8,128)(2,1)S(1)}, u32[]{:S(2)}, u32[]{:S(2)}) %collective-permute-start.4) | collective-permute-done | bytes 655392 | tf_op jit(solution)/shard_map/cond/branch_0_fun/ppermute | solution.py:157
  167.5 0.0 collective-permute-done.3
  167.5 0.9 broadcast_select_fusion.1
  168.5 2.0 %collective-permute-start.5 = (bf16[20,16,1024]{2,1,0:T(8,128)(2,1)}, bf16[20,16,1024]{2,1,0:T(8,128)(2,1)}, u32[]{:S(2)}, u32[]{:S(2)}) collective-permute-start(bf16[20,16,1024]{2,1,0:T(8,128)(2,1)} %broadcast_select_fusion.1), channel_id=1, source_target_pairs={{0,16},{1,49},{16,32},{17,1},{32,48},{33,17},{48,0},{49,33},{2,18}... | collective-permute-start | bytes 1966088 | tf_op jit(solution)/shard_map/cond/branch_0_fun/ppermute | solution.py:164
  170.5 0.1 pad_add_fusion.1.refs_0_
  170.6 0.1 pad_add_fusion.refs_0_
  170.6 0.0 all-gather.7.cloned.1.call-done
  170.6 0.0 copy-start.2
  170.6 1.7 copy-done.2
  172.4 0.0 copy-start.3
  172.4 3.3 %branch_0_fun.5.refs_6_ = f32[512,1024]{1,0:T(8,128)S(1)} custom-call(s32[3]{0:T(128)S(1)} %pad_add_fusion.1.refs_0_, bf16[8,320,512]{2,1,0:T(8,128)(2,1)S(1)} %bitcast.85, bf16[320,1024]{1,0:T(8,128)(2,1)} %bitcast.14.refs_2_, bf16[320,1024]{1,0:T(8,128)(2,1)S(1)} %bitcast.90, bf16[320,1024]{1,0:T(8,128)(2,1)S(1)} %bitcast.91), custom_call_target="tpu_custom_call" | custom-call | flops 1006632960 | bytes 5046272 | tf_op jit(solution)/shard_map/cond/branch_0_fun/pallas_call | solution.py:128
  175.6 0.0 collective-permute-done.8
  175.7 0.0 copy-done.3
  175.7 3.7 %branch_0_fun.6.refs_3_ = f32[512,1024]{1,0:T(8,128)S(1)} custom-call(s32[4]{0:T(128)S(1)} %pad_add_fusion.refs_0_, bf16[8,320,512]{2,1,0:T(8,128)(2,1)S(1)} %bitcast.86, bf16[320,1024]{1,0:T(8,128)(2,1)} %bitcast.7.refs_2_, bf16[320,1024]{1,0:T(8,128)(2,1)S(1)} %bitcast.92, bf16[320,1024]{1,0:T(8,128)(2,1)S(1)} %bitcast.89, bf16[320,1024]{1,0:T(8,128)(2,1)S(1)} %bitcast.88, ...), custom_call_target="tpu_custom_call" | custom-call | flops 1342177280 | bytes 6029312 | tf_op jit(solution)/shard_map/cond/branch_0_fun/pallas_call | solution.py:128
  179.3 2.0 %collective-permute-done.5 = bf16[20,16,1024]{2,1,0:T(8,128)(2,1)} collective-permute-done((bf16[20,16,1024]{2,1,0:T(8,128)(2,1)}, bf16[20,16,1024]{2,1,0:T(8,128)(2,1)}, u32[]{:S(2)}, u32[]{:S(2)}) %collective-permute-start.5) | collective-permute-done | bytes 655392 | tf_op jit(solution)/shard_map/cond/branch_0_fun/ppermute | solution.py:164
  181.3 2.0 %branch_0_fun.7 = bf16[512,1024]{1,0:T(8,128)(2,1)S(1)} custom-call(s32[1]{0:T(128)} %bitcast.refs_0_, bf16[8,320,512]{2,1,0:T(8,128)(2,1)S(1)} %bitcast.87, bf16[320,1024]{1,0:T(8,128)(2,1)} %bitcast.2.refs_2_, f32[512,1024]{1,0:T(8,128)S(1)} %branch_0_fun.6.refs_3_), custom_call_target="tpu_custom_call" | custom-call | flops 335544320 | bytes 3080192 | tf_op jit(solution)/shard_map/cond/branch_0_fun/pallas_call | solution.py:128
  183.5 0.0 copy-start.6
  183.5 1.0 copy-done.6
  (4 shorter events, 0.1 us)
Async XLA Ops:
  10.7 12.2 %copy-start.7 = (s32[1,64,2]{1,2,0:T(2,128)S(1)}, s32[1,64,2]{1,2,0:T(2,128)}, u32[]{:S(2)}) copy-start(s32[1,64,2]{1,2,0:T(2,128)} %param.9) | copy-start | bytes 1540
  10.7 85.5 %all-to-all-start = ((bf16[64,16,1536]{2,1,0:T(8,128)(2,1)}), bf16[64,16,1536]{2,1,0:T(8,128)(2,1)S(1)}, u32[]{:S(2)}, u32[]{:S(2)}) async-start(bf16[64,16,1536]{2,1,0:T(8,128)(2,1)} %shard_map.39), calls=%async_computation | async-start | bytes 6291456 | tf_op jit(solution)/shard_map/all_to_all | solution.py:190
  23.0 4.5 %collective-permute-start.18 = (s32[1,64,2]{1,2,0:T(2,128)S(1)}, s32[1,64,2]{1,2,0:T(2,128)S(1)}, u32[]{:S(2)}, u32[]{:S(2)}) collective-permute-start(s32[1,64,2]{1,2,0:T(2,128)S(1)} %copy-done.7), channel_id=1, source_target_pairs={{0,64},{64,128},{128,192},{192,0},{1,65},{65,129},{129,193},{193,1... | collective-permute-start | bytes 1544 | tf_op jit(solution)/shard_map/ppermute | solution.py:184
  23.5 4.8 %collective-permute-start.20 = (s32[1,64,2]{1,2,0:T(2,128)S(1)}, s32[1,64,2]{1,2,0:T(2,128)S(1)}, u32[]{:S(2)}, u32[]{:S(2)}) collective-permute-start(s32[1,64,2]{1,2,0:T(2,128)S(1)} %copy-done.7), channel_id=1, source_target_pairs={{0,192},{64,0},{128,64},{192,128},{1,193},{65,1},{129,65},{193,129... | collective-permute-start | bytes 1544 | tf_op jit(solution)/shard_map/ppermute | solution.py:184
  25.1 5.1 %collective-permute-start.19 = (s32[1,64,2]{1,2,0:T(2,128)S(1)}, s32[1,64,2]{1,2,0:T(2,128)S(1)}, u32[]{:S(2)}, u32[]{:S(2)}) collective-permute-start(s32[1,64,2]{1,2,0:T(2,128)S(1)} %copy-done.7), channel_id=1, source_target_pairs={{0,128},{64,192},{128,0},{192,64},{1,129},{65,193},{129,1},{193,65... | collective-permute-start | bytes 1544 | tf_op jit(solution)/shard_map/ppermute | solution.py:184
  96.3 74.4 %all-gather.7.cloned.1.call-start = ((), (), s32[]{:S(2)}) async-start(), calls=%async_computation.1 | async-start | bytes 2949120 | tf_op jit(solution)/shard_map/cond/branch_0_fun/all_gather | solution.py:153
  99.9 18.4 %collective-permute-start = (bf16[20,16,1024]{2,1,0:T(8,128)(2,1)}, bf16[20,16,1024]{2,1,0:T(8,128)(2,1)S(1)}, u32[]{:S(2)}, u32[]{:S(2)}) collective-permute-start(bf16[20,16,1024]{2,1,0:T(8,128)(2,1)} %get-tuple-element.168), channel_id=1, source_target_pairs={{0,4},{1,13},{2,6},{3,15},{4,8},{5,1},{6,10},{7,3},{8,12},{9,5},{1... | collective-permute-start | bytes 1966088 | tf_op jit(solution)/shard_map/cond/branch_0_fun/ppermute | solution.py:147
  101.2 18.4 %collective-permute-start.1 = (bf16[20,16,1024]{2,1,0:T(8,128)(2,1)}, bf16[20,16,1024]{2,1,0:T(8,128)(2,1)}, u32[]{:S(2)}, u32[]{:S(2)}) collective-permute-start(bf16[20,16,1024]{2,1,0:T(8,128)(2,1)} %get-tuple-element.168), channel_id=1, source_target_pairs={{0,192},{64,0},{128,64},{192,128},{1,193},{65,1},{129,65},{193,129... | collective-permute-start | bytes 1966088 | tf_op jit(solution)/shard_map/cond/branch_0_fun/ppermute | solution.py:144
  119.6 25.4 %collective-permute-start.2 = (bf16[20,16,1024]{2,1,0:T(8,128)(2,1)S(1)}, bf16[20,16,1024]{2,1,0:T(8,128)(2,1)S(1)}, u32[]{:S(2)}, u32[]{:S(2)}) collective-permute-start(bf16[20,16,1024]{2,1,0:T(8,128)(2,1)S(1)} %collective-permute-done), channel_id=1, source_target_pairs={{0,196},{1,205},{2,198},{3,207},{4,200},{5,193},{6,202},{7,195},{8... | collective-permute-start | bytes 1966088 | tf_op jit(solution)/shard_map/cond/branch_0_fun/ppermute | solution.py:149
  120.1 31.8 %collective-permute-start.6 = (bf16[20,16,1024]{2,1,0:T(8,128)(2,1)}, bf16[20,16,1024]{2,1,0:T(8,128)(2,1)S(1)}, u32[]{:S(2)}, u32[]{:S(2)}) collective-permute-start(bf16[20,16,1024]{2,1,0:T(8,128)(2,1)} %collective-permute-done.1), channel_id=1, source_target_pairs={{0,16},{16,32},{32,48},{48,0},{1,17},{17,33},{33,49},{49,1},{2,18}... | collective-permute-start | bytes 1966088 | tf_op jit(solution)/shard_map/cond/branch_0_fun/ppermute | solution.py:156
  121.4 30.5 %collective-permute-start.7 = (bf16[20,16,1024]{2,1,0:T(8,128)(2,1)}, bf16[20,16,1024]{2,1,0:T(8,128)(2,1)S(1)}, u32[]{:S(2)}, u32[]{:S(2)}) collective-permute-start(bf16[20,16,1024]{2,1,0:T(8,128)(2,1)} %collective-permute-done.1), channel_id=1, source_target_pairs={{0,48},{16,0},{32,16},{48,32},{1,49},{17,1},{33,17},{49,33},{2,50}... | collective-permute-start | bytes 1966088 | tf_op jit(solution)/shard_map/cond/branch_0_fun/ppermute | solution.py:157
  145.0 22.5 %collective-permute-start.4 = (bf16[20,16,1024]{2,1,0:T(8,128)(2,1)S(1)}, bf16[20,16,1024]{2,1,0:T(8,128)(2,1)S(1)}, u32[]{:S(2)}, u32[]{:S(2)}) collective-permute-start(bf16[20,16,1024]{2,1,0:T(8,128)(2,1)S(1)} %collective-permute-done.2), channel_id=1, source_target_pairs={{0,48},{16,0},{32,16},{48,32},{1,49},{17,1},{33,17},{49,33},{2,50}... | collective-permute-start | bytes 1966088 | tf_op jit(solution)/shard_map/cond/branch_0_fun/ppermute | solution.py:157
  148.3 19.2 %collective-permute-start.3 = (bf16[20,16,1024]{2,1,0:T(8,128)(2,1)S(1)}, bf16[20,16,1024]{2,1,0:T(8,128)(2,1)S(1)}, u32[]{:S(2)}, u32[]{:S(2)}) collective-permute-start(bf16[20,16,1024]{2,1,0:T(8,128)(2,1)S(1)} %collective-permute-done.2), channel_id=1, source_target_pairs={{0,16},{16,32},{32,48},{48,0},{1,17},{17,33},{33,49},{49,1},{2,18}... | collective-permute-start | bytes 1966088 | tf_op jit(solution)/shard_map/cond/branch_0_fun/ppermute | solution.py:156
  152.8 22.8 %collective-permute-start.8 = (bf16[20,16,1024]{2,1,0:T(8,128)(2,1)}, bf16[20,16,1024]{2,1,0:T(8,128)(2,1)}, u32[]{:S(2)}, u32[]{:S(2)}) collective-permute-start(bf16[20,16,1024]{2,1,0:T(8,128)(2,1)} %broadcast_select_fusion), channel_id=1, source_target_pairs={{0,16},{1,49},{16,32},{17,1},{32,48},{33,17},{48,0},{49,33},{2,18}... | collective-permute-start | bytes 1966088 | tf_op jit(solution)/shard_map/cond/branch_0_fun/ppermute | solution.py:164
  168.5 12.8 %collective-permute-start.5 = (bf16[20,16,1024]{2,1,0:T(8,128)(2,1)}, bf16[20,16,1024]{2,1,0:T(8,128)(2,1)}, u32[]{:S(2)}, u32[]{:S(2)}) collective-permute-start(bf16[20,16,1024]{2,1,0:T(8,128)(2,1)} %broadcast_select_fusion.1), channel_id=1, source_target_pairs={{0,16},{1,49},{16,32},{17,1},{32,48},{33,17},{48,0},{49,33},{2,18}... | collective-permute-start | bytes 1966088 | tf_op jit(solution)/shard_map/cond/branch_0_fun/ppermute | solution.py:164
  170.6 1.7 copy-start.2
  172.4 3.3 %copy-start.3 = (bf16[160,16,512]{2,1,0:T(8,128)(2,1)S(1)}, bf16[160,16,512]{2,1,0:T(8,128)(2,1)}, u32[]{:S(2)}) copy-start(bf16[160,16,512]{2,1,0:T(8,128)(2,1)} %all-gather.7.cloned.1.call-done) | copy-start | bytes 7864324 | tf_op jit(solution)/shard_map/cond
  183.5 1.0 copy-start.6
Sparse Core Ops, SparseCore 0:
  119.7 43.7 all-gather.6
where the time goes:
time: 192 us; the launch traced here: 191 us
  waiting for transfers between devices  118 us (61%)
  starting transfers between devices  32.5 us (17%)
  Pallas kernels  16.1 us (8%)
  between operations  15.9 us (8%)
  other arithmetic  5.1 us (3%)
  local copies, waits for them, and re-layouts  2.72 us (1%)
    all_to_all x1, waiting for transfers between devices, shards(): recv = lax.all_to_all(packed, DP, split_axis=0, concat_axis=0, tiled=True)  63.4 us
    ppermute x1, waiting for transfers between devices, gather_and_multiply(): lax.ppermute(far, ('x', 'zh', 'zl', 'core'), [(s * 2 * NZ + i, (s - 1) %...  21.7 us
    ppermute x1, waiting for transfers between devices, gather_and_multiply(): far = lax.ppermute(grads_c, ('zh', 'zl', 'core'), hop)  16.3 us
    ppermute x2, waiting for transfers between devices, beside(): down = lax.ppermute(own, 'y', ring('y', NY, -1))  12.7 us
    all_to_all x1, starting transfers between devices, shards(): recv = lax.all_to_all(packed, DP, split_axis=0, concat_axis=0, tiled=True)  12.2 us
    pallas_call x3, Pallas kernels, products(): pl.pallas_call(lambda *refs: product_kernel(len(pieces), scale, total is...  8.93 us
    ppermute x2, starting transfers between devices, beside(): down = lax.ppermute(own, 'y', ring('y', NY, -1))  5.3 us
    ppermute x2, starting transfers between devices, beside(): up = lax.ppermute(own, 'y', ring('y', NY, 1))  4.8 us
  transfers between devices with their start and end apart: 14, of which 8 were waited for; matrix products, arithmetic and copies ran while one was open for 3% of the time, Pallas kernels for 4%

commit v1 on v0

--- a/solution.py
+++ b/solution.py
@@ -29,7 +29,7 @@
 
 
 def pack_kernel(acts_ref, grads_ref, out_ref):
-    for a in range(2):
+    for a in range(4):
         for c in range(HGRID):
             out_ref[a * HGRID + c, :, :TR] = acts_ref[c * SUB:(c + 1) * SUB, a * TR:(a + 1) * TR]
             out_ref[a * HGRID + c, :, TR:] = grads_ref[a * SUB:(a + 1) * SUB, c * TC:(c + 1) * TC]
@@ -38,12 +38,12 @@
 def pack(acts, grads):
     return pl.pallas_call(
         pack_kernel,
-        grid=(DGRID // 2,),
+        grid=(DGRID // 4,),
         in_specs=[
-            pl.BlockSpec((BLOCK, 2 * TR), lambda a: (0, a)),
-            pl.BlockSpec((2 * SUB, HW), lambda a: (a, 0)),
+            pl.BlockSpec((BLOCK, 4 * TR), lambda a: (0, a)),
+            pl.BlockSpec((4 * SUB, HW), lambda a: (a, 0)),
         ],
-        out_specs=pl.BlockSpec((2 * HGRID, SUB, TR + TC), lambda a: (a, 0, 0)),
+        out_specs=pl.BlockSpec((4 * HGRID, SUB, TR + TC), lambda a: (a, 0, 0)),
         out_shape=jax.ShapeDtypeStruct((DGRID * HGRID, SUB, TR + TC), jnp.bfloat16),
     )(acts, grads)
 
@@ -141,10 +141,10 @@
 def gather_and_multiply(cap, recv, aidx, gidx, count, total, dtype, scale):
     y, zh, core = lax.axis_index("y"), lax.axis_index("zh"), lax.axis_index("core")
     acts_c, grads_c = compact(cap, recv, aidx, gidx, count)
-    near = lax.ppermute(grads_c, "x", ring("x", NX, -1))
     plane = [(z, c) for z in range(NZ) for c in range(2)]
     hop = [((z * 2 + c), (z + (2 if c == 0 else -2)) % NZ * 2 + c) for z, c in plane]
     far = lax.ppermute(grads_c, ("zh", "zl", "core"), hop)
+    near = lax.ppermute(grads_c, "x", ring("x", NX, -1))
     far, near, acts_c = lax.optimization_barrier((far, near, acts_c))
     far = lax.ppermute(
         far, ("x", "zh", "zl", "core"),
@@ -186,7 +186,7 @@
     touched = [jnp.any(b[0] == 0, axis=1) for b in behind]
     counts = [jnp.sum(t.astype(jnp.int32)) for t in touched]
     most = jnp.maximum(jnp.maximum(counts[0], counts[1]), jnp.maximum(counts[2], counts[3]))
-    aidx, gidx = order_of(touched[0]), order_of(touched[1])
+    aidx, gidx = (jnp.pad(order_of(t), (0, MORE)) for t in touched[:2])
     recv = lax.all_to_all(packed, DP, split_axis=0, concat_axis=0, tiled=True)
 
     scale = 2.0 / math.sqrt(BLOCKS * BLOCK)

time: 192 us -> 191 us (level)
  transfers between devices with their start and end apart: 14 -> 14, of which waited for: 8 -> 7; matrix products, arithmetic and copies ran while one was open for 3% -> 3% of each run, Pallas kernels for 4% -> 4%
where the time goes in v1:
time: 191 us; the launch traced here: 190 us
  waiting for transfers between devices  118 us (62%)
  starting transfers between devices  32.7 us (17%)
  between operations  15.9 us (8%)
  Pallas kernels  15 us (8%)
  other arithmetic  5.11 us (3%)
  local copies, waits for them, and re-layouts  2.72 us (1%)
    all_to_all x1, waiting for transfers between devices, shards(): recv = lax.all_to_all(packed, DP, split_axis=0, concat_axis=0, tiled=True)  63.6 us
    ppermute x1, waiting for transfers between devices, gather_and_multiply(): lax.ppermute(far, ('x', 'zh', 'zl', 'core'), [(s * 2 * NZ + i, (s - 1) %...  21.6 us
    ppermute x1, waiting for transfers between devices, gather_and_multiply(): far = lax.ppermute(grads_c, ('zh', 'zl', 'core'), hop)  16.3 us
    ppermute x2, waiting for transfers between devices, beside(): down = lax.ppermute(own, 'y', ring('y', NY, -1))  12.7 us
    all_to_all x1, starting transfers between devices, shards(): recv = lax.all_to_all(packed, DP, split_axis=0, concat_axis=0, tiled=True)  12.2 us
    pallas_call x3, Pallas kernels, products(): pl.pallas_call(lambda *refs: product_kernel(len(pieces), scale, total is...  8.93 us
    ppermute x2, starting transfers between devices, beside(): down = lax.ppermute(own, 'y', ring('y', NY, -1))  5.3 us
    ppermute x2, starting transfers between devices, beside(): up = lax.ppermute(own, 'y', ring('y', NY, 1))  4.8 us
  transfers between devices with their start and end apart: 14, of which 7 were waited for; matrix products, arithmetic and copies ran while one was open for 3% of the time, Pallas kernels for 4%

profile of v1, /device:TPU:6, one launch (start us, length us, event | category | flops | bytes accessed | tf_op | source)
XLA Modules:
  0.0 190.2 jit_solution(2586542746389942584)
XLA Ops:
  6.5 3.1 %shard_map.39 = bf16[64,16,1536]{2,1,0:T(8,128)(2,1)} custom-call(bf16[128,4096]{1,0:T(8,128)(2,1)} %bitcast.95, bf16[128,8192]{1,0:T(8,128)(2,1)} %bitcast.93), custom_call_target="tpu_custom_call" | custom-call | tf_op jit(solution)/shard_map/pallas_call | solution.py:39
  9.7 0.0 copy-start.7
  9.7 12.2 %all-to-all-start = ((bf16[64,16,1536]{2,1,0:T(8,128)(2,1)}), bf16[64,16,1536]{2,1,0:T(8,128)(2,1)S(1)}, u32[]{:S(2)}, u32[]{:S(2)}) async-start(bf16[64,16,1536]{2,1,0:T(8,128)(2,1)} %shard_map.39), calls=%async_computation | async-start | bytes 6291456 | tf_op jit(solution)/shard_map/all_to_all | solution.py:190
  21.9 0.0 copy-done.7
  21.9 0.6 collective-permute-start.18
  22.5 1.5 collective-permute-start.20
  24.0 1.4 collective-permute-start.19
  25.5 0.1 convert_reduce_fusion.1
  25.6 0.1 select_reduce_fusion.1
  25.7 0.7 convert_reduce_fusion.5
  26.4 0.0 collective-permute-done.18
  26.4 0.1 convert_reduce_fusion
  26.5 0.1 select_reduce_fusion
  26.7 0.6 convert_reduce_fusion.4
  27.3 0.0 collective-permute-done.20
  28.6 0.5 collective-permute-done.19
  29.1 0.6 convert_reduce_fusion.2
  29.8 0.6 convert_reduce_fusion.3
  31.6 63.6 %all-to-all-done = bf16[64,16,1536]{2,1,0:T(8,128)(2,1)S(1)} async-done(((bf16[64,16,1536]{2,1,0:T(8,128)(2,1)}), bf16[64,16,1536]{2,1,0:T(8,128)(2,1)S(1)}, u32[]{:S(2)}, u32[]{:S(2)}) %all-to-all-start) | async-done | bytes 3145760 | tf_op jit(solution)/shard_map/all_to_all | solution.py:190
  95.2 87.2 %conditional.1 = (bf16[1,1,512,1024]{3,2,1,0:T(8,128)(2,1)S(1)}) conditional(s32[]{:T(128)} %clamp.3, (s32[92]{0:T(128)S(1)}, s32[92]{0:T(128)S(1)}, s32[1]{0:T(128)}, bf16[64,16,1536]{2,1,0:T(8,128)(2,1)S(1)}) %tuple.35, (s32[]{:T(128)}, s32[92]{0:T(128)S(1)}, s32[92]{0:T(128)S(1)}, s32[1]{0:T(128)}, bf16[64,16,1536]{2,1,0:T(8,128)(2,1)S(1)}) %tuple.36), branch_computations={%region_12.13_spmd, %region_13.16_spmd} | conditional | flops 3760062464 | bytes 127993888 | solution.py:215
  95.2 0.0 all-gather.7.cloned.1.call-start
  95.9 2.9 %branch_0_fun.4 = (bf16[20,16,512]{2,1,0:T(8,128)(2,1)}, bf16[20,16,1024]{2,1,0:T(8,128)(2,1)}) custom-call(s32[20]{0:T(128)S(1)} %bitcast.96, s32[20]{0:T(128)S(1)} %bitcast.97, s32[1]{0:T(128)S(6)} %min.8.refs_2_, bf16[64,16,1536]{2,1,0:T(8,128)(2,1)S(1)} %get-tuple-element.167.refs_3_), custom_call_target="tpu_custom_call" | custom-call | tf_op jit(solution)/shard_map/cond/branch_0_fun/pallas_call | solution.py:81
  98.8 1.3 collective-permute-start
  100.1 0.9 collective-permute-start.1
  100.9 16.3 %collective-permute-done = bf16[20,16,1024]{2,1,0:T(8,128)(2,1)S(1)} collective-permute-done((bf16[20,16,1024]{2,1,0:T(8,128)(2,1)}, bf16[20,16,1024]{2,1,0:T(8,128)(2,1)S(1)}, u32[]{:S(2)}, u32[]{:S(2)}) %collective-permute-start) | collective-permute-done | bytes 655392 | tf_op jit(solution)/shard_map/cond/branch_0_fun/ppermute | solution.py:146
  117.2 1.2 collective-permute-done.1
  118.5 0.0 all-gather.7.cloned.1.call-update
  118.5 0.6 collective-permute-start.2
  119.1 1.2 collective-permute-start.6
  120.3 2.0 %collective-permute-start.7 = (bf16[20,16,1024]{2,1,0:T(8,128)(2,1)}, bf16[20,16,1024]{2,1,0:T(8,128)(2,1)S(1)}, u32[]{:S(2)}, u32[]{:S(2)}) collective-permute-start(bf16[20,16,1024]{2,1,0:T(8,128)(2,1)} %collective-permute-done.1), channel_id=1, source_target_pairs={{0,48},{16,0},{32,16},{48,32},{1,49},{17,1},{33,17},{49,33},{2,50}... | collective-permute-start | bytes 1966088 | tf_op jit(solution)/shard_map/cond/branch_0_fun/ppermute | solution.py:157
  122.4 21.6 %collective-permute-done.2 = bf16[20,16,1024]{2,1,0:T(8,128)(2,1)S(1)} collective-permute-done((bf16[20,16,1024]{2,1,0:T(8,128)(2,1)S(1)}, bf16[20,16,1024]{2,1,0:T(8,128)(2,1)S(1)}, u32[]{:S(2)}, u32[]{:S(2)}) %collective-permute-start.2) | collective-permute-done | bytes 655392 | tf_op jit(solution)/shard_map/cond/branch_0_fun/ppermute | solution.py:149
  143.9 3.3 %collective-permute-start.4 = (bf16[20,16,1024]{2,1,0:T(8,128)(2,1)S(1)}, bf16[20,16,1024]{2,1,0:T(8,128)(2,1)S(1)}, u32[]{:S(2)}, u32[]{:S(2)}) collective-permute-start(bf16[20,16,1024]{2,1,0:T(8,128)(2,1)S(1)} %collective-permute-done.2), channel_id=1, source_target_pairs={{0,48},{16,0},{32,16},{48,32},{1,49},{17,1},{33,17},{49,33},{2,50}... | collective-permute-start | bytes 1966088 | tf_op jit(solution)/shard_map/cond/branch_0_fun/ppermute | solution.py:157
  147.2 3.6 %collective-permute-start.3 = (bf16[20,16,1024]{2,1,0:T(8,128)(2,1)S(1)}, bf16[20,16,1024]{2,1,0:T(8,128)(2,1)S(1)}, u32[]{:S(2)}, u32[]{:S(2)}) collective-permute-start(bf16[20,16,1024]{2,1,0:T(8,128)(2,1)S(1)} %collective-permute-done.2), channel_id=1, source_target_pairs={{0,16},{16,32},{32,48},{48,0},{1,17},{17,33},{33,49},{49,1},{2,18}... | collective-permute-start | bytes 1966088 | tf_op jit(solution)/shard_map/cond/branch_0_fun/ppermute | solution.py:156
  150.8 0.0 collective-permute-done.6
  150.8 0.0 collective-permute-done.7
  150.8 0.9 broadcast_select_fusion
  151.7 2.0 %collective-permute-start.8 = (bf16[20,16,1024]{2,1,0:T(8,128)(2,1)}, bf16[20,16,1024]{2,1,0:T(8,128)(2,1)}, u32[]{:S(2)}, u32[]{:S(2)}) collective-permute-start(bf16[20,16,1024]{2,1,0:T(8,128)(2,1)} %broadcast_select_fusion), channel_id=1, source_target_pairs={{0,16},{1,49},{16,32},{17,1},{32,48},{33,17},{48,0},{49,33},{2,18}... | collective-permute-start | bytes 1966088 | tf_op jit(solution)/shard_map/cond/branch_0_fun/ppermute | solution.py:164
  153.8 12.7 %collective-permute-done.4 = bf16[20,16,1024]{2,1,0:T(8,128)(2,1)S(1)} collective-permute-done((bf16[20,16,1024]{2,1,0:T(8,128)(2,1)S(1)}, bf16[20,16,1024]{2,1,0:T(8,128)(2,1)S(1)}, u32[]{:S(2)}, u32[]{:S(2)}) %collective-permute-start.4) | collective-permute-done | bytes 655392 | tf_op jit(solution)/shard_map/cond/branch_0_fun/ppermute | solution.py:157
  166.5 0.0 collective-permute-done.3
  166.5 0.9 broadcast_select_fusion.1
  167.4 2.0 %collective-permute-start.5 = (bf16[20,16,1024]{2,1,0:T(8,128)(2,1)}, bf16[20,16,1024]{2,1,0:T(8,128)(2,1)}, u32[]{:S(2)}, u32[]{:S(2)}) collective-permute-start(bf16[20,16,1024]{2,1,0:T(8,128)(2,1)} %broadcast_select_fusion.1), channel_id=1, source_target_pairs={{0,16},{1,49},{16,32},{17,1},{32,48},{33,17},{48,0},{49,33},{2,18}... | collective-permute-start | bytes 1966088 | tf_op jit(solution)/shard_map/cond/branch_0_fun/ppermute | solution.py:164
  169.4 0.1 pad_add_fusion.1.refs_0_
  169.5 0.1 pad_add_fusion.refs_0_
  169.5 0.0 all-gather.7.cloned.1.call-done
  169.5 0.0 copy-start.2
  169.5 1.7 copy-done.2
  171.3 0.0 copy-start.3
  171.3 3.3 %branch_0_fun.5.refs_6_ = f32[512,1024]{1,0:T(8,128)S(1)} custom-call(s32[3]{0:T(128)S(1)} %pad_add_fusion.1.refs_0_, bf16[8,320,512]{2,1,0:T(8,128)(2,1)S(1)} %bitcast.85, bf16[320,1024]{1,0:T(8,128)(2,1)} %bitcast.14.refs_2_, bf16[320,1024]{1,0:T(8,128)(2,1)S(1)} %bitcast.90, bf16[320,1024]{1,0:T(8,128)(2,1)S(1)} %bitcast.91), custom_call_target="tpu_custom_call" | custom-call | flops 1006632960 | bytes 5046272 | tf_op jit(solution)/shard_map/cond/branch_0_fun/pallas_call | solution.py:128
  174.6 0.0 collective-permute-done.8
  174.6 0.0 copy-done.3
  174.6 3.7 %branch_0_fun.6.refs_3_ = f32[512,1024]{1,0:T(8,128)S(1)} custom-call(s32[4]{0:T(128)S(1)} %pad_add_fusion.refs_0_, bf16[8,320,512]{2,1,0:T(8,128)(2,1)S(1)} %bitcast.86, bf16[320,1024]{1,0:T(8,128)(2,1)} %bitcast.7.refs_2_, bf16[320,1024]{1,0:T(8,128)(2,1)S(1)} %bitcast.92, bf16[320,1024]{1,0:T(8,128)(2,1)S(1)} %bitcast.89, bf16[320,1024]{1,0:T(8,128)(2,1)S(1)} %bitcast.88, ...), custom_call_target="tpu_custom_call" | custom-call | flops 1342177280 | bytes 6029312 | tf_op jit(solution)/shard_map/cond/branch_0_fun/pallas_call | solution.py:128
  178.2 2.0 %collective-permute-done.5 = bf16[20,16,1024]{2,1,0:T(8,128)(2,1)} collective-permute-done((bf16[20,16,1024]{2,1,0:T(8,128)(2,1)}, bf16[20,16,1024]{2,1,0:T(8,128)(2,1)}, u32[]{:S(2)}, u32[]{:S(2)}) %collective-permute-start.5) | collective-permute-done | bytes 655392 | tf_op jit(solution)/shard_map/cond/branch_0_fun/ppermute | solution.py:164
  180.2 2.0 %branch_0_fun.7 = bf16[512,1024]{1,0:T(8,128)(2,1)S(1)} custom-call(s32[1]{0:T(128)} %bitcast.refs_0_, bf16[8,320,512]{2,1,0:T(8,128)(2,1)S(1)} %bitcast.87, bf16[320,1024]{1,0:T(8,128)(2,1)} %bitcast.2.refs_2_, f32[512,1024]{1,0:T(8,128)S(1)} %branch_0_fun.6.refs_3_), custom_call_target="tpu_custom_call" | custom-call | flops 335544320 | bytes 3080192 | tf_op jit(solution)/shard_map/cond/branch_0_fun/pallas_call | solution.py:128
  182.4 0.0 copy-start.6
  182.4 1.0 copy-done.6
  (6 shorter events, 0.1 us)
Async XLA Ops:
  9.7 12.2 %copy-start.7 = (s32[1,64,2]{1,2,0:T(2,128)S(1)}, s32[1,64,2]{1,2,0:T(2,128)}, u32[]{:S(2)}) copy-start(s32[1,64,2]{1,2,0:T(2,128)} %param.9) | copy-start | bytes 1540
  9.7 85.5 %all-to-all-start = ((bf16[64,16,1536]{2,1,0:T(8,128)(2,1)}), bf16[64,16,1536]{2,1,0:T(8,128)(2,1)S(1)}, u32[]{:S(2)}, u32[]{:S(2)}) async-start(bf16[64,16,1536]{2,1,0:T(8,128)(2,1)} %shard_map.39), calls=%async_computation | async-start | bytes 6291456 | tf_op jit(solution)/shard_map/all_to_all | solution.py:190
  21.9 4.5 %collective-permute-start.18 = (s32[1,64,2]{1,2,0:T(2,128)S(1)}, s32[1,64,2]{1,2,0:T(2,128)S(1)}, u32[]{:S(2)}, u32[]{:S(2)}) collective-permute-start(s32[1,64,2]{1,2,0:T(2,128)S(1)} %copy-done.7), channel_id=1, source_target_pairs={{0,64},{64,128},{128,192},{192,0},{1,65},{65,129},{129,193},{193,1... | collective-permute-start | bytes 1544 | tf_op jit(solution)/shard_map/ppermute | solution.py:184
  22.5 4.8 %collective-permute-start.20 = (s32[1,64,2]{1,2,0:T(2,128)S(1)}, s32[1,64,2]{1,2,0:T(2,128)S(1)}, u32[]{:S(2)}, u32[]{:S(2)}) collective-permute-start(s32[1,64,2]{1,2,0:T(2,128)S(1)} %copy-done.7), channel_id=1, source_target_pairs={{0,192},{64,0},{128,64},{192,128},{1,193},{65,1},{129,65},{193,129... | collective-permute-start | bytes 1544 | tf_op jit(solution)/shard_map/ppermute | solution.py:184
  24.0 5.1 %collective-permute-start.19 = (s32[1,64,2]{1,2,0:T(2,128)S(1)}, s32[1,64,2]{1,2,0:T(2,128)S(1)}, u32[]{:S(2)}, u32[]{:S(2)}) collective-permute-start(s32[1,64,2]{1,2,0:T(2,128)S(1)} %copy-done.7), channel_id=1, source_target_pairs={{0,128},{64,192},{128,0},{192,64},{1,129},{65,193},{129,1},{193,65... | collective-permute-start | bytes 1544 | tf_op jit(solution)/shard_map/ppermute | solution.py:184
  95.2 74.3 %all-gather.7.cloned.1.call-start = ((), (), s32[]{:S(2)}) async-start(), calls=%async_computation.1 | async-start | bytes 2949120 | tf_op jit(solution)/shard_map/cond/branch_0_fun/all_gather | solution.py:153
  98.8 18.4 %collective-permute-start = (bf16[20,16,1024]{2,1,0:T(8,128)(2,1)}, bf16[20,16,1024]{2,1,0:T(8,128)(2,1)S(1)}, u32[]{:S(2)}, u32[]{:S(2)}) collective-permute-start(bf16[20,16,1024]{2,1,0:T(8,128)(2,1)} %get-tuple-element.168), channel_id=1, source_target_pairs={{0,4},{1,13},{2,6},{3,15},{4,8},{5,1},{6,10},{7,3},{8,12},{9,5},{1... | collective-permute-start | bytes 1966088 | tf_op jit(solution)/shard_map/cond/branch_0_fun/ppermute | solution.py:146
  100.1 18.4 %collective-permute-start.1 = (bf16[20,16,1024]{2,1,0:T(8,128)(2,1)}, bf16[20,16,1024]{2,1,0:T(8,128)(2,1)}, u32[]{:S(2)}, u32[]{:S(2)}) collective-permute-start(bf16[20,16,1024]{2,1,0:T(8,128)(2,1)} %get-tuple-element.168), channel_id=1, source_target_pairs={{0,192},{64,0},{128,64},{192,128},{1,193},{65,1},{129,65},{193,129... | collective-permute-start | bytes 1966088 | tf_op jit(solution)/shard_map/cond/branch_0_fun/ppermute | solution.py:147
  118.5 25.4 %collective-permute-start.2 = (bf16[20,16,1024]{2,1,0:T(8,128)(2,1)S(1)}, bf16[20,16,1024]{2,1,0:T(8,128)(2,1)S(1)}, u32[]{:S(2)}, u32[]{:S(2)}) collective-permute-start(bf16[20,16,1024]{2,1,0:T(8,128)(2,1)S(1)} %collective-permute-done), channel_id=1, source_target_pairs={{0,196},{1,205},{2,198},{3,207},{4,200},{5,193},{6,202},{7,195},{8... | collective-permute-start | bytes 1966088 | tf_op jit(solution)/shard_map/cond/branch_0_fun/ppermute | solution.py:149
  119.1 31.7 %collective-permute-start.6 = (bf16[20,16,1024]{2,1,0:T(8,128)(2,1)}, bf16[20,16,1024]{2,1,0:T(8,128)(2,1)S(1)}, u32[]{:S(2)}, u32[]{:S(2)}) collective-permute-start(bf16[20,16,1024]{2,1,0:T(8,128)(2,1)} %collective-permute-done.1), channel_id=1, source_target_pairs={{0,16},{16,32},{32,48},{48,0},{1,17},{17,33},{33,49},{49,1},{2,18}... | collective-permute-start | bytes 1966088 | tf_op jit(solution)/shard_map/cond/branch_0_fun/ppermute | solution.py:156
  120.3 30.5 %collective-permute-start.7 = (bf16[20,16,1024]{2,1,0:T(8,128)(2,1)}, bf16[20,16,1024]{2,1,0:T(8,128)(2,1)S(1)}, u32[]{:S(2)}, u32[]{:S(2)}) collective-permute-start(bf16[20,16,1024]{2,1,0:T(8,128)(2,1)} %collective-permute-done.1), channel_id=1, source_target_pairs={{0,48},{16,0},{32,16},{48,32},{1,49},{17,1},{33,17},{49,33},{2,50}... | collective-permute-start | bytes 1966088 | tf_op jit(solution)/shard_map/cond/branch_0_fun/ppermute | solution.py:157
  143.9 22.5 %collective-permute-start.4 = (bf16[20,16,1024]{2,1,0:T(8,128)(2,1)S(1)}, bf16[20,16,1024]{2,1,0:T(8,128)(2,1)S(1)}, u32[]{:S(2)}, u32[]{:S(2)}) collective-permute-start(bf16[20,16,1024]{2,1,0:T(8,128)(2,1)S(1)} %collective-permute-done.2), channel_id=1, source_target_pairs={{0,48},{16,0},{32,16},{48,32},{1,49},{17,1},{33,17},{49,33},{2,50}... | collective-permute-start | bytes 1966088 | tf_op jit(solution)/shard_map/cond/branch_0_fun/ppermute | solution.py:157
  147.2 19.2 %collective-permute-start.3 = (bf16[20,16,1024]{2,1,0:T(8,128)(2,1)S(1)}, bf16[20,16,1024]{2,1,0:T(8,128)(2,1)S(1)}, u32[]{:S(2)}, u32[]{:S(2)}) collective-permute-start(bf16[20,16,1024]{2,1,0:T(8,128)(2,1)S(1)} %collective-permute-done.2), channel_id=1, source_target_pairs={{0,16},{16,32},{32,48},{48,0},{1,17},{17,33},{33,49},{49,1},{2,18}... | collective-permute-start | bytes 1966088 | tf_op jit(solution)/shard_map/cond/branch_0_fun/ppermute | solution.py:156
  151.7 22.8 %collective-permute-start.8 = (bf16[20,16,1024]{2,1,0:T(8,128)(2,1)}, bf16[20,16,1024]{2,1,0:T(8,128)(2,1)}, u32[]{:S(2)}, u32[]{:S(2)}) collective-permute-start(bf16[20,16,1024]{2,1,0:T(8,128)(2,1)} %broadcast_select_fusion), channel_id=1, source_target_pairs={{0,16},{1,49},{16,32},{17,1},{32,48},{33,17},{48,0},{49,33},{2,18}... | collective-permute-start | bytes 1966088 | tf_op jit(solution)/shard_map/cond/branch_0_fun/ppermute | solution.py:164
  167.4 12.8 %collective-permute-start.5 = (bf16[20,16,1024]{2,1,0:T(8,128)(2,1)}, bf16[20,16,1024]{2,1,0:T(8,128)(2,1)}, u32[]{:S(2)}, u32[]{:S(2)}) collective-permute-start(bf16[20,16,1024]{2,1,0:T(8,128)(2,1)} %broadcast_select_fusion.1), channel_id=1, source_target_pairs={{0,16},{1,49},{16,32},{17,1},{32,48},{33,17},{48,0},{49,33},{2,18}... | collective-permute-start | bytes 1966088 | tf_op jit(solution)/shard_map/cond/branch_0_fun/ppermute | solution.py:164
  169.5 1.7 copy-start.2
  171.3 3.3 %copy-start.3 = (bf16[160,16,512]{2,1,0:T(8,128)(2,1)S(1)}, bf16[160,16,512]{2,1,0:T(8,128)(2,1)}, u32[]{:S(2)}) copy-start(bf16[160,16,512]{2,1,0:T(8,128)(2,1)} %all-gather.7.cloned.1.call-done) | copy-start | bytes 7864324 | tf_op jit(solution)/shard_map/cond
  182.4 1.0 copy-start.6
Sparse Core Ops, SparseCore 0:
  118.6 43.7 all-gather.6

commit v2 on v1

--- a/solution.py
+++ b/solution.py
@@ -24,7 +24,7 @@
 MTILE = 256
 
 MAIN = 20
-MORE = 28
+MORE = 32
 DP = ("y", "zh", "zl", "core")
 
 

time: 191 us -> 239 us (1.25)
  waiting for transfers between devices: 118 us -> 158 us
  Pallas kernels: 15 us -> 19.5 us
  local copies, waits for them, and re-layouts: 2.72 us -> 6.34 us
  starting transfers between devices: 32.7 us -> 29.1 us
    ppermute x1, waiting for transfers between devices: 1.25 us -> 24.8 us  [gather_and_multiply(): near = lax.ppermute(grads_c, 'x', ring('x', NX, -1))]
    ppermute x2, waiting for transfers between devices: 0.01 us -> 20.1 us  [beside(): up = lax.ppermute(own, 'y', ring('y', NY, 1))]
    ppermute x1, waiting for transfers between devices: 16.3 us -> 1 us  [gather_and_multiply(): far = lax.ppermute(grads_c, ('zh', 'zl', 'core'), hop)]
    ppermute x1, waiting for transfers between devices: 21.6 us -> 36.3 us  [gather_and_multiply(): lax.ppermute(far, ('x', 'zh', 'zl', 'core'), [(s * 2 * NZ + i, (s - 1) %...]
    ppermute x2, waiting for transfers between devices: 12.7 us -> 2.25 us  [beside(): down = lax.ppermute(own, 'y', ring('y', NY, -1))]
    ppermute x2, waiting for transfers between devices: 1.96 us -> 9.51 us  [across(): return lax.ppermute(jnp.where(core == 0, up, down), DP, pairs)]
    pallas_call x3, Pallas kernels: 8.93 us -> 12.3 us  [products(): pl.pallas_call(lambda *refs: product_kernel(len(pieces), scale, total is...]
    ppermute x2, starting transfers between devices: 5.3 us -> 2.73 us  [beside(): down = lax.ppermute(own, 'y', ring('y', NY, -1))]
  transfers between devices with their start and end apart: 14 -> 14, of which waited for: 7 -> 9; matrix products, arithmetic and copies ran while one was open for 3% -> 2% of each run, Pallas kernels for 4% -> 4%
where the time goes in v2:
time: 239 us; the launch traced here: 237 us
  waiting for transfers between devices  158 us (66%)
  starting transfers between devices  29.1 us (12%)
  Pallas kernels  19.5 us (8%)
  between operations  16 us (7%)
  other arithmetic  7.34 us (3%)
  local copies, waits for them, and re-layouts  6.34 us (3%)
    all_to_all x1, waiting for transfers between devices, shards(): recv = lax.all_to_all(packed, DP, split_axis=0, concat_axis=0, tiled=True)  63.6 us
    ppermute x1, waiting for transfers between devices, gather_and_multiply(): lax.ppermute(far, ('x', 'zh', 'zl', 'core'), [(s * 2 * NZ + i, (s - 1) %...  36.3 us
    ppermute x1, waiting for transfers between devices, gather_and_multiply(): near = lax.ppermute(grads_c, 'x', ring('x', NX, -1))  24.8 us
    ppermute x2, waiting for transfers between devices, beside(): up = lax.ppermute(own, 'y', ring('y', NY, 1))  20.1 us
    pallas_call x3, Pallas kernels, products(): pl.pallas_call(lambda *refs: product_kernel(len(pieces), scale, total is...  12.3 us
    all_to_all x1, starting transfers between devices, shards(): recv = lax.all_to_all(packed, DP, split_axis=0, concat_axis=0, tiled=True)  12.2 us
    ppermute x2, waiting for transfers between devices, across(): return lax.ppermute(jnp.where(core == 0, up, down), DP, pairs)  9.51 us
    ppermute x2, starting transfers between devices, beside(): up = lax.ppermute(own, 'y', ring('y', NY, 1))  5.1 us
  transfers between devices with their start and end apart: 14, of which 9 were waited for; matrix products, arithmetic and copies ran while one was open for 2% of the time, Pallas kernels for 4%

profile of v2, /device:TPU:6, one launch (start us, length us, event | category | flops | bytes accessed | tf_op | source)
XLA Modules:
  0.0 237.1 jit_solution(120690925481426396)
XLA Ops:
  6.5 3.1 %shard_map.39 = bf16[64,16,1536]{2,1,0:T(8,128)(2,1)} custom-call(bf16[128,4096]{1,0:T(8,128)(2,1)} %bitcast.95, bf16[128,8192]{1,0:T(8,128)(2,1)} %bitcast.93), custom_call_target="tpu_custom_call" | custom-call | tf_op jit(solution)/shard_map/pallas_call | solution.py:39
  9.7 0.0 copy-start.7
  9.7 12.2 %all-to-all-start = ((bf16[64,16,1536]{2,1,0:T(8,128)(2,1)}), bf16[64,16,1536]{2,1,0:T(8,128)(2,1)S(1)}, u32[]{:S(2)}, u32[]{:S(2)}) async-start(bf16[64,16,1536]{2,1,0:T(8,128)(2,1)} %shard_map.39), calls=%async_computation | async-start | bytes 6291456 | tf_op jit(solution)/shard_map/all_to_all | solution.py:190
  21.9 0.0 copy-done.7
  21.9 0.6 collective-permute-start.18
  22.5 1.5 collective-permute-start.20
  24.0 1.4 collective-permute-start.19
  25.5 0.1 convert_reduce_fusion.1
  25.6 0.1 select_reduce_fusion.1
  25.7 0.7 convert_reduce_fusion.5
  26.4 0.0 collective-permute-done.18
  26.4 0.1 convert_reduce_fusion
  26.5 0.1 select_reduce_fusion
  26.7 0.6 convert_reduce_fusion.4
  27.3 0.0 collective-permute-done.20
  28.7 0.4 collective-permute-done.19
  29.1 0.6 convert_reduce_fusion.2
  29.8 0.6 convert_reduce_fusion.3
  31.6 63.6 %all-to-all-done = bf16[64,16,1536]{2,1,0:T(8,128)(2,1)S(1)} async-done(((bf16[64,16,1536]{2,1,0:T(8,128)(2,1)}), bf16[64,16,1536]{2,1,0:T(8,128)(2,1)S(1)}, u32[]{:S(2)}, u32[]{:S(2)}) %all-to-all-start) | async-done | bytes 3145760 | tf_op jit(solution)/shard_map/all_to_all | solution.py:190
  95.2 134.0 %conditional.1 = (bf16[1,1,512,1024]{3,2,1,0:T(8,128)(2,1)S(1)}) conditional(s32[]{:T(128)} %clamp.3, (s32[96]{0:T(128)S(1)}, s32[96]{0:T(128)S(1)}, s32[1]{0:T(128)}, bf16[64,16,1536]{2,1,0:T(8,128)(2,1)S(1)}) %tuple.35, (s32[]{:T(128)}, s32[96]{0:T(128)S(1)}, s32[96]{0:T(128)S(1)}, s32[1]{0:T(128)}, bf16[64,16,1536]{2,1,0:T(8,128)(2,1)S(1)}) %tuple.36), branch_computations={%region_12.13_spmd, %region_13.16_spmd} | conditional | flops 4297064448 | bytes 141035712 | solution.py:215
  95.2 1.6 broadcast.24
  96.9 130.5 %while.13 = (s32[]{:T(128)}, f32[512,1024]{1,0:T(8,128)}, s32[]{:T(128)}, s32[96]{0:T(128)S(1)}, s32[96]{0:T(128)S(1)}, /*index=5*/s32[1]{0:T(128)}, bf16[64,16,...) while((s32[]{:T(128)}, f32[512,1024]{1,0:T(8,128)}, ...), condition=%wide.region_15.15_spmd, body=%wide.region_14.14_spmd.sunk | while | flops 4296015872 | bytes 135792496 | solution.py:212
  96.9 0.0 copy-start.4
  96.9 0.0 all-gather.9.cloned.1.call-start
  96.9 0.7 dynamic_slice.8.refs_0_
  97.6 0.8 dynamic_slice.9.refs_1_
  99.1 4.1 %body.16 = (bf16[32,16,512]{2,1,0:T(8,128)(2,1)}, bf16[32,16,1024]{2,1,0:T(8,128)(2,1)}) custom-call(s32[32]{0:T(128)} %dynamic_slice.8.refs_0_, s32[32]{0:T(128)} %dynamic_slice.9.refs_1_, s32[1]{0:T(128)S(6)} %min.11.refs_2_, bf16[64,16,1536]{2,1,0:T(8,128)(2,1)S(1)} %get-tuple-element.306.refs_3_), custom_call_target="tpu_custom_call" | custom-call | tf_op jit(solution)/shard_map/cond/branch_1_fun/while/body/pallas_call | solution.py:81
  103.2 0.9 collective-permute-start.10
  104.2 1.2 collective-permute-start.9
  105.4 24.8 %collective-permute-done.10 = bf16[32,16,1024]{2,1,0:T(8,128)(2,1)} collective-permute-done((bf16[32,16,1024]{2,1,0:T(8,128)(2,1)}, bf16[32,16,1024]{2,1,0:T(8,128)(2,1)}, u32[]{:S(2)}, u32[]{:S(2)}) %collective-permute-start.10) | collective-permute-done | bytes 1048608 | tf_op jit(solution)/shard_map/cond/branch_1_fun/while/body/ppermute | solution.py:147
  130.2 1.0 collective-permute-done.9
  131.1 0.0 all-gather.9.cloned.1.call-update
  131.2 0.0 copy-done.4
  131.2 1.6 collective-permute-start.11
  132.8 0.8 collective-permute-start.15
  133.6 2.4 %collective-permute-start.16 = (bf16[32,16,1024]{2,1,0:T(8,128)(2,1)}, bf16[32,16,1024]{2,1,0:T(8,128)(2,1)S(1)}, u32[]{:S(2)}, u32[]{:S(2)}) collective-permute-start(bf16[32,16,1024]{2,1,0:T(8,128)(2,1)} %collective-permute-done.10), channel_id=1, source_target_pairs={{0,48},{16,0},{32,16},{48,32},{1,49},{17,1},{33,17},{49,33},{2,50}... | collective-permute-start | bytes 3145736 | tf_op jit(solution)/shard_map/cond/branch_1_fun/while/body/ppermute | solution.py:157
  136.0 36.3 %collective-permute-done.11 = bf16[32,16,1024]{2,1,0:T(8,128)(2,1)} collective-permute-done((bf16[32,16,1024]{2,1,0:T(8,128)(2,1)}, bf16[32,16,1024]{2,1,0:T(8,128)(2,1)}, u32[]{:S(2)}, u32[]{:S(2)}) %collective-permute-start.11) | collective-permute-done | bytes 1048608 | tf_op jit(solution)/shard_map/cond/branch_1_fun/while/body/ppermute | solution.py:149
  172.3 4.3 %collective-permute-start.12 = (bf16[32,16,1024]{2,1,0:T(8,128)(2,1)}, bf16[32,16,1024]{2,1,0:T(8,128)(2,1)S(1)}, u32[]{:S(2)}, u32[]{:S(2)}) collective-permute-start(bf16[32,16,1024]{2,1,0:T(8,128)(2,1)} %collective-permute-done.11), channel_id=1, source_target_pairs={{0,16},{16,32},{32,48},{48,0},{1,17},{17,33},{33,49},{49,1},{2,18}... | collective-permute-start | bytes 3145736 | tf_op jit(solution)/shard_map/cond/branch_1_fun/while/body/ppermute | solution.py:156
  176.6 0.3 collective-permute-start.13
  176.9 0.0 collective-permute-done.15
  176.9 0.0 collective-permute-done.16
  176.9 1.1 broadcast_select_fusion.7
  178.0 1.7 collective-permute-start.17
  179.7 20.1 %collective-permute-done.12 = bf16[32,16,1024]{2,1,0:T(8,128)(2,1)S(1)} collective-permute-done((bf16[32,16,1024]{2,1,0:T(8,128)(2,1)}, bf16[32,16,1024]{2,1,0:T(8,128)(2,1)S(1)}, u32[]{:S(2)}, u32[]{:S(2)}) %collective-permute-start.12) | collective-permute-done | bytes 1048608 | tf_op jit(solution)/shard_map/cond/branch_1_fun/while/body/ppermute | solution.py:156
  199.8 2.3 collective-permute-done.13
  202.1 1.1 broadcast_select_fusion.6
  203.1 0.1 collective-permute-start.14
  203.3 0.1 pad_add_fusion.7.refs_0_
  203.3 0.1 pad_add_fusion.6.refs_0_
  203.4 0.0 all-gather.9.cloned.1.call-done
  203.4 0.0 copy-start
  203.4 2.2 copy-done
  205.6 0.0 copy-start.1
  205.6 4.1 %body.17.refs_6_ = f32[512,1024]{1,0:T(8,128)S(1)} custom-call(s32[3]{0:T(128)S(1)} %pad_add_fusion.7.refs_0_, bf16[8,512,512]{2,1,0:T(8,128)(2,1)S(1)} %bitcast.79, bf16[512,1024]{1,0:T(8,128)(2,1)} %bitcast.76.refs_2_, bf16[512,1024]{1,0:T(8,128)(2,1)S(1)} %bitcast.82, bf16[512,1024]{1,0:T(8,128)(2,1)S(1)} %bitcast.83, f32[512,1024]{1,0:T(8,128)} %get-tuple-element.282.refs_5_), custom_call_target="tpu_custom_call" | custom-call | flops 1610612736 | bytes 6815744 | tf_op jit(solution)/shard_map/cond/branch_1_fun/while/body/pallas_call | solution.py:128
  209.7 2.7 %collective-permute-done.17 = bf16[32,16,1024]{2,1,0:T(8,128)(2,1)} collective-permute-done((bf16[32,16,1024]{2,1,0:T(8,128)(2,1)}, bf16[32,16,1024]{2,1,0:T(8,128)(2,1)}, u32[]{:S(2)}, u32[]{:S(2)}) %collective-permute-start.17) | collective-permute-done | bytes 1048608 | tf_op jit(solution)/shard_map/cond/branch_1_fun/while/body/ppermute | solution.py:164
  212.5 0.0 copy-done.1
  212.5 4.5 %body.18.refs_3_ = f32[512,1024]{1,0:T(8,128)S(1)} custom-call(s32[4]{0:T(128)S(1)} %pad_add_fusion.6.refs_0_, bf16[8,512,512]{2,1,0:T(8,128)(2,1)S(1)} %bitcast.80, bf16[512,1024]{1,0:T(8,128)(2,1)} %bitcast.69.refs_2_, bf16[512,1024]{1,0:T(8,128)(2,1)} %bitcast.70.refs_3_, bf16[512,1024]{1,0:T(8,128)(2,1)S(1)} %bitcast.84, ...), custom_call_target="tpu_custom_call" | custom-call | flops 2147483648 | bytes 8388608 | tf_op jit(solution)/shard_map/cond/branch_1_fun/while/body/pallas_call | solution.py:128
  216.9 6.8 %collective-permute-done.14 = bf16[32,16,1024]{2,1,0:T(8,128)(2,1)} collective-permute-done((bf16[32,16,1024]{2,1,0:T(8,128)(2,1)}, bf16[32,16,1024]{2,1,0:T(8,128)(2,1)}, u32[]{:S(2)}, u32[]{:S(2)}) %collective-permute-start.14) | collective-permute-done | bytes 1048608 | tf_op jit(solution)/shard_map/cond/branch_1_fun/while/body/ppermute | solution.py:164
  223.7 0.0 copy-start.5
  223.7 3.7 %body.19 = f32[512,1024]{1,0:T(8,128)} custom-call(s32[1]{0:T(128)} %bitcast.61.refs_0_, bf16[8,512,512]{2,1,0:T(8,128)(2,1)S(1)} %bitcast.81, bf16[512,1024]{1,0:T(8,128)(2,1)} %bitcast.64.refs_2_, f32[512,1024]{1,0:T(8,128)S(1)} %body.18.refs_3_), custom_call_target="tpu_custom_call" | custom-call | flops 536870912 | bytes 3670016 | tf_op jit(solution)/shard_map/cond/branch_1_fun/while/body/pallas_call | solution.py:128
  227.4 0.0 copy-done.5
  227.4 1.8 fusion
  229.3 0.0 copy-start.6
  229.3 1.0 copy-done.6
  (6 shorter events, 0.1 us)
Async XLA Ops:
  9.7 12.2 %copy-start.7 = (s32[1,64,2]{1,2,0:T(2,128)S(1)}, s32[1,64,2]{1,2,0:T(2,128)}, u32[]{:S(2)}) copy-start(s32[1,64,2]{1,2,0:T(2,128)} %param.9) | copy-start | bytes 1540
  9.7 85.5 %all-to-all-start = ((bf16[64,16,1536]{2,1,0:T(8,128)(2,1)}), bf16[64,16,1536]{2,1,0:T(8,128)(2,1)S(1)}, u32[]{:S(2)}, u32[]{:S(2)}) async-start(bf16[64,16,1536]{2,1,0:T(8,128)(2,1)} %shard_map.39), calls=%async_computation | async-start | bytes 6291456 | tf_op jit(solution)/shard_map/all_to_all | solution.py:190
  21.9 4.5 %collective-permute-start.18 = (s32[1,64,2]{1,2,0:T(2,128)S(1)}, s32[1,64,2]{1,2,0:T(2,128)S(1)}, u32[]{:S(2)}, u32[]{:S(2)}) collective-permute-start(s32[1,64,2]{1,2,0:T(2,128)S(1)} %copy-done.7), channel_id=1, source_target_pairs={{0,64},{64,128},{128,192},{192,0},{1,65},{65,129},{129,193},{193,1... | collective-permute-start | bytes 1544 | tf_op jit(solution)/shard_map/ppermute | solution.py:184
  22.5 4.8 %collective-permute-start.20 = (s32[1,64,2]{1,2,0:T(2,128)S(1)}, s32[1,64,2]{1,2,0:T(2,128)S(1)}, u32[]{:S(2)}, u32[]{:S(2)}) collective-permute-start(s32[1,64,2]{1,2,0:T(2,128)S(1)} %copy-done.7), channel_id=1, source_target_pairs={{0,192},{64,0},{128,64},{192,128},{1,193},{65,1},{129,65},{193,129... | collective-permute-start | bytes 1544 | tf_op jit(solution)/shard_map/ppermute | solution.py:184
  24.0 5.1 %collective-permute-start.19 = (s32[1,64,2]{1,2,0:T(2,128)S(1)}, s32[1,64,2]{1,2,0:T(2,128)S(1)}, u32[]{:S(2)}, u32[]{:S(2)}) collective-permute-start(s32[1,64,2]{1,2,0:T(2,128)S(1)} %copy-done.7), channel_id=1, source_target_pairs={{0,128},{64,192},{128,0},{192,64},{1,129},{65,193},{129,1},{193,65... | collective-permute-start | bytes 1544 | tf_op jit(solution)/shard_map/ppermute | solution.py:184
  96.9 34.3 %copy-start.4 = (bf16[64,16,1536]{2,1,0:T(8,128)(2,1)}, bf16[64,16,1536]{2,1,0:T(8,128)(2,1)S(1)}, u32[]{:S(2)}) copy-start(bf16[64,16,1536]{2,1,0:T(8,128)(2,1)S(1)} %get-tuple-element.306.refs_3_) | copy-start | bytes 9437188 | tf_op jit(solution)/shard_map/cond/branch_1_fun/while
  96.9 106.6 %all-gather.9.cloned.1.call-start = ((), (), s32[]{:S(2)}) async-start(), calls=%async_computation.2 | async-start | bytes 4718592 | tf_op jit(solution)/shard_map/cond/branch_1_fun/while/body/all_gather | solution.py:153
  103.2 26.9 %collective-permute-start.10 = (bf16[32,16,1024]{2,1,0:T(8,128)(2,1)}, bf16[32,16,1024]{2,1,0:T(8,128)(2,1)}, u32[]{:S(2)}, u32[]{:S(2)}) collective-permute-start(bf16[32,16,1024]{2,1,0:T(8,128)(2,1)} %get-tuple-element.257), channel_id=1, source_target_pairs={{0,192},{64,0},{128,64},{192,128},{1,193},{65,1},{129,65},{193,129... | collective-permute-start | bytes 3145736 | tf_op jit(solution)/shard_map/cond/branch_1_fun/while/body/ppermute | solution.py:147
  104.2 27.0 %collective-permute-start.9 = (bf16[32,16,1024]{2,1,0:T(8,128)(2,1)}, bf16[32,16,1024]{2,1,0:T(8,128)(2,1)}, u32[]{:S(2)}, u32[]{:S(2)}) collective-permute-start(bf16[32,16,1024]{2,1,0:T(8,128)(2,1)} %get-tuple-element.257), channel_id=1, source_target_pairs={{0,4},{1,13},{2,6},{3,15},{4,8},{5,1},{6,10},{7,3},{8,12},{9,5},{1... | collective-permute-start | bytes 3145736 | tf_op jit(solution)/shard_map/cond/branch_1_fun/while/body/ppermute | solution.py:146
  131.2 41.1 %collective-permute-start.11 = (bf16[32,16,1024]{2,1,0:T(8,128)(2,1)}, bf16[32,16,1024]{2,1,0:T(8,128)(2,1)}, u32[]{:S(2)}, u32[]{:S(2)}) collective-permute-start(bf16[32,16,1024]{2,1,0:T(8,128)(2,1)} %collective-permute-done.9), channel_id=1, source_target_pairs={{0,196},{1,205},{2,198},{3,207},{4,200},{5,193},{6,202},{7,195},{8... | collective-permute-start | bytes 3145736 | tf_op jit(solution)/shard_map/cond/branch_1_fun/while/body/ppermute | solution.py:149
  132.8 44.1 %collective-permute-start.15 = (bf16[32,16,1024]{2,1,0:T(8,128)(2,1)}, bf16[32,16,1024]{2,1,0:T(8,128)(2,1)S(1)}, u32[]{:S(2)}, u32[]{:S(2)}) collective-permute-start(bf16[32,16,1024]{2,1,0:T(8,128)(2,1)} %collective-permute-done.10), channel_id=1, source_target_pairs={{0,16},{16,32},{32,48},{48,0},{1,17},{17,33},{33,49},{49,1},{2,18}... | collective-permute-start | bytes 3145736 | tf_op jit(solution)/shard_map/cond/branch_1_fun/while/body/ppermute | solution.py:156
  133.6 43.3 %collective-permute-start.16 = (bf16[32,16,1024]{2,1,0:T(8,128)(2,1)}, bf16[32,16,1024]{2,1,0:T(8,128)(2,1)S(1)}, u32[]{:S(2)}, u32[]{:S(2)}) collective-permute-start(bf16[32,16,1024]{2,1,0:T(8,128)(2,1)} %collective-permute-done.10), channel_id=1, source_target_pairs={{0,48},{16,0},{32,16},{48,32},{1,49},{17,1},{33,17},{49,33},{2,50}... | collective-permute-start | bytes 3145736 | tf_op jit(solution)/shard_map/cond/branch_1_fun/while/body/ppermute | solution.py:157
  172.3 27.5 %collective-permute-start.12 = (bf16[32,16,1024]{2,1,0:T(8,128)(2,1)}, bf16[32,16,1024]{2,1,0:T(8,128)(2,1)S(1)}, u32[]{:S(2)}, u32[]{:S(2)}) collective-permute-start(bf16[32,16,1024]{2,1,0:T(8,128)(2,1)} %collective-permute-done.11), channel_id=1, source_target_pairs={{0,16},{16,32},{32,48},{48,0},{1,17},{17,33},{33,49},{49,1},{2,18}... | collective-permute-start | bytes 3145736 | tf_op jit(solution)/shard_map/cond/branch_1_fun/while/body/ppermute | solution.py:156
  176.6 25.5 %collective-permute-start.13 = (bf16[32,16,1024]{2,1,0:T(8,128)(2,1)}, bf16[32,16,1024]{2,1,0:T(8,128)(2,1)}, u32[]{:S(2)}, u32[]{:S(2)}) collective-permute-start(bf16[32,16,1024]{2,1,0:T(8,128)(2,1)} %collective-permute-done.11), channel_id=1, source_target_pairs={{0,48},{16,0},{32,16},{48,32},{1,49},{17,1},{33,17},{49,33},{2,50}... | collective-permute-start | bytes 3145736 | tf_op jit(solution)/shard_map/cond/branch_1_fun/while/body/ppermute | solution.py:157
  178.0 34.4 %collective-permute-start.17 = (bf16[32,16,1024]{2,1,0:T(8,128)(2,1)}, bf16[32,16,1024]{2,1,0:T(8,128)(2,1)}, u32[]{:S(2)}, u32[]{:S(2)}) collective-permute-start(bf16[32,16,1024]{2,1,0:T(8,128)(2,1)} %broadcast_select_fusion.7), channel_id=1, source_target_pairs={{0,16},{1,49},{16,32},{17,1},{32,48},{33,17},{48,0},{49,33},{2,18}... | collective-permute-start | bytes 3145736 | tf_op jit(solution)/shard_map/cond/branch_1_fun/while/body/ppermute | solution.py:164
  203.1 20.6 %collective-permute-start.14 = (bf16[32,16,1024]{2,1,0:T(8,128)(2,1)}, bf16[32,16,1024]{2,1,0:T(8,128)(2,1)}, u32[]{:S(2)}, u32[]{:S(2)}) collective-permute-start(bf16[32,16,1024]{2,1,0:T(8,128)(2,1)} %broadcast_select_fusion.6), channel_id=1, source_target_pairs={{0,16},{1,49},{16,32},{17,1},{32,48},{33,17},{48,0},{49,33},{2,18}... | collective-permute-start | bytes 3145736 | tf_op jit(solution)/shard_map/cond/branch_1_fun/while/body/ppermute | solution.py:164
  203.4 2.2 copy-start
  205.6 6.8 %copy-start.1 = (bf16[256,16,512]{2,1,0:T(8,128)(2,1)S(1)}, bf16[256,16,512]{2,1,0:T(8,128)(2,1)}, u32[]{:S(2)}) copy-start(bf16[256,16,512]{2,1,0:T(8,128)(2,1)} %all-gather.9.cloned.1.call-done) | copy-start | bytes 12582916 | tf_op jit(solution)/shard_map/cond/branch_1_fun/while
  223.7 3.7 %copy-start.5 = (bf16[64,16,1536]{2,1,0:T(8,128)(2,1)S(1)}, bf16[64,16,1536]{2,1,0:T(8,128)(2,1)}, u32[]{:S(2)}) copy-start(bf16[64,16,1536]{2,1,0:T(8,128)(2,1)} %copy-done.4) | copy-start | bytes 9437188 | tf_op jit(solution)/shard_map/cond/branch_1_fun/while
  229.3 1.0 copy-start.6
Sparse Core Ops, SparseCore 0:
  131.3 64.8 all-gather.8

commit v3 on v2

--- a/solution.py
+++ b/solution.py
@@ -152,29 +152,32 @@
     )
     acts_all = lax.all_gather(acts_c, ("zl", "core")).reshape(DGRID, cap * SUB, TR)
 
-    def beside(own):
-        up = lax.ppermute(own, "y", ring("y", NY, 1))
-        down = lax.ppermute(own, "y", ring("y", NY, -1))
-        return up, down
-
-    def across(up, down):
-        way = [(yy * 2 + c, (yy + (1 if c == 0 else -1)) % NY * 2 + c) for yy in range(NY) for c in range(2)]
-        pairs = [(i // 2 * 2 * NZ + i % 2, j // 2 * 2 * NZ + j % 2) for i, j in way]
-        pairs = [(i + 2 * z, j + 2 * z) for z in range(NZ) for i, j in pairs]
-        return lax.ppermute(jnp.where(core == 0, up, down), DP, pairs)
+    def ring_step(sign):
+        return [
+            ((yy * NZ + z) * 2 + c, ((yy + (sign if c == 0 else -sign)) % NY * NZ + z) * 2 + c)
+            for yy in range(NY) for z in range(NZ) for c in range(2)
+        ]
+
+    def around(own):
+        first = lax.ppermute(own, DP, ring_step(1))
+        second = lax.ppermute(own, DP, ring_step(-1))
+        third = lax.ppermute(first, DP, ring_step(1))
+        return first, second, third
 
     def places(flip):
         h = 1 - zh if flip else zh
-        return jnp.stack([lax.rem(y + NY - d, NY) * 2 + h for d in (0, 1, 3, 2)]).astype(jnp.int32)
-
-    up, down = beside(near)
-    third = across(up, down)
-    far_up, far_down = beside(far)
-    far_third = across(far_up, far_down)
+        way = 1 - 2 * core
+        return jnp.stack(
+            [lax.rem(y + NY - d, NY) * 2 + h for d in (0, way, -way, 2)]
+        ).astype(jnp.int32)
+
+    first, second, third = around(near)
+    far, second = lax.optimization_barrier((far, second))
+    far_first, far_second, far_third = around(far)
     here, there = places(False), places(True)
-    total = products(here[:3], acts_all, (near, up, down), total, jnp.float32)
-    both = jnp.concatenate([here[3:], there[:3]])
-    total = products(both, acts_all, (third, far, far_up, far_down), total, jnp.float32)
+    most = jnp.concatenate([here, there[:3]])
+    pieces = (near, first, second, third, far, far_first, far_second)
+    total = products(most, acts_all, pieces, total, jnp.float32)
     return products(there[3:], acts_all, (far_third,), total, dtype, scale)
 
 

time: 239 us -> 240 us (level)
  other arithmetic: 7.34 us -> 4.91 us
    pallas_call x3 -> x2, Pallas kernels: 12.3 us -> 10.9 us  [products(): pl.pallas_call(lambda *refs: product_kernel(len(pieces), scale, total is...]
  transfers between devices with their start and end apart: 14 -> 14, of which waited for: 9 -> 9; matrix products, arithmetic and copies ran while one was open for 2% -> 1% of each run, Pallas kernels for 4% -> 3%
where the time goes in v3:
time: 240 us; the launch traced here: 237 us
  waiting for transfers between devices  159 us (66%)
  starting transfers between devices  31.4 us (13%)
  Pallas kernels  18.2 us (8%)
  between operations  15.9 us (7%)
  local copies, waits for them, and re-layouts  6.48 us (3%)
  other arithmetic  4.91 us (2%)
    all_to_all x1, waiting for transfers between devices, shards(): recv = lax.all_to_all(packed, DP, split_axis=0, concat_axis=0, tiled=True)  63.6 us
    ppermute x1, waiting for transfers between devices, gather_and_multiply(): lax.ppermute(far, ('x', 'zh', 'zl', 'core'), [(s * 2 * NZ + i, (s - 1) %...  37.6 us
    ppermute x1, waiting for transfers between devices, gather_and_multiply(): near = lax.ppermute(grads_c, 'x', ring('x', NX, -1))  24.7 us
    ppermute x2, waiting for transfers between devices, around(): first = lax.ppermute(own, DP, ring_step(1))  16.1 us
    ppermute x2, waiting for transfers between devices, around(): third = lax.ppermute(first, DP, ring_step(1))  15.4 us
    all_to_all x1, starting transfers between devices, shards(): recv = lax.all_to_all(packed, DP, split_axis=0, concat_axis=0, tiled=True)  12.2 us
    pallas_call x2, Pallas kernels, products(): pl.pallas_call(lambda *refs: product_kernel(len(pieces), scale, total is...  10.9 us
    ppermute x2, starting transfers between devices, around(): first = lax.ppermute(own, DP, ring_step(1))  5.49 us
  transfers between devices with their start and end apart: 14, of which 9 were waited for; matrix products, arithmetic and copies ran while one was open for 1% of the time, Pallas kernels for 3%

profile of v3, /device:TPU:6, one launch (start us, length us, event | category | flops | bytes accessed | tf_op | source)
XLA Modules:
  0.0 236.7 jit_solution(7665904116667204995)
XLA Ops:
  6.5 3.1 %shard_map.39 = bf16[64,16,1536]{2,1,0:T(8,128)(2,1)} custom-call(bf16[128,4096]{1,0:T(8,128)(2,1)} %bitcast.93, bf16[128,8192]{1,0:T(8,128)(2,1)} %bitcast.91), custom_call_target="tpu_custom_call" | custom-call | tf_op jit(solution)/shard_map/pallas_call | solution.py:39
  9.7 0.0 copy-start.7
  9.7 12.2 %all-to-all-start = ((bf16[64,16,1536]{2,1,0:T(8,128)(2,1)}), bf16[64,16,1536]{2,1,0:T(8,128)(2,1)S(1)}, u32[]{:S(2)}, u32[]{:S(2)}) async-start(bf16[64,16,1536]{2,1,0:T(8,128)(2,1)} %shard_map.39), calls=%async_computation | async-start | bytes 6291456 | tf_op jit(solution)/shard_map/all_to_all | solution.py:193
  21.9 0.0 copy-done.7
  21.9 0.6 collective-permute-start.18
  22.5 1.5 collective-permute-start.20
  24.0 1.4 collective-permute-start.19
  25.5 0.1 convert_reduce_fusion.1
  25.6 0.1 select_reduce_fusion.1
  25.7 0.6 convert_reduce_fusion.5
  26.3 0.0 collective-permute-done.18
  26.3 0.1 convert_reduce_fusion
  26.5 0.1 select_reduce_fusion
  26.6 0.6 convert_reduce_fusion.4
  27.2 0.1 collective-permute-done.20
  28.5 0.6 collective-permute-done.19
  29.1 0.6 convert_reduce_fusion.2
  29.8 0.6 convert_reduce_fusion.3
  31.6 63.6 %all-to-all-done = bf16[64,16,1536]{2,1,0:T(8,128)(2,1)S(1)} async-done(((bf16[64,16,1536]{2,1,0:T(8,128)(2,1)}), bf16[64,16,1536]{2,1,0:T(8,128)(2,1)S(1)}, u32[]{:S(2)}, u32[]{:S(2)}) %all-to-all-start) | async-done | bytes 3145760 | tf_op jit(solution)/shard_map/all_to_all | solution.py:193
  95.2 133.7 %conditional.1 = (bf16[1,1,512,1024]{3,2,1,0:T(8,128)(2,1)S(1)}) conditional(s32[]{:T(128)} %clamp.3, (s32[96]{0:T(128)S(1)}, s32[96]{0:T(128)S(1)}, s32[1]{0:T(128)}, bf16[64,16,1536]{2,1,0:T(8,128)(2,1)S(1)}) %tuple.37, (s32[]{:T(128)}, s32[96]{0:T(128)S(1)}, s32[96]{0:T(128)S(1)}, s32[1]{0:T(128)}, bf16[64,16,1536]{2,1,0:T(8,128)(2,1)S(1)}) %tuple.38), branch_computations={%region_12.13_spmd, %region_13.16_spmd} | conditional | flops 4296015872 | bytes 132647112 | solution.py:218
  95.2 1.6 broadcast.24
  96.9 130.2 %while.13 = (s32[]{:T(128)}, f32[512,1024]{1,0:T(8,128)}, s32[]{:T(128)}, s32[96]{0:T(128)S(1)}, s32[96]{0:T(128)S(1)}, /*index=5*/s32[1]{0:T(128)}, bf16[64,16,...) while((s32[]{:T(128)}, f32[512,1024]{1,0:T(8,128)}, ...), condition=%wide.region_15.15_spmd, body=%wide.region_14.14_spmd.sunk | while | flops 4294967296 | bytes 127403896 | solution.py:215
  96.9 0.0 copy-start.4
  96.9 0.0 all-gather.9.cloned.1.call-start
  96.9 0.8 dynamic_slice.9.refs_1_
  97.6 0.8 dynamic_slice.8.refs_0_
  99.0 4.1 %body.15 = (bf16[32,16,512]{2,1,0:T(8,128)(2,1)}, bf16[32,16,1024]{2,1,0:T(8,128)(2,1)}) custom-call(s32[32]{0:T(128)} %dynamic_slice.8.refs_0_, s32[32]{0:T(128)} %dynamic_slice.9.refs_1_, s32[1]{0:T(128)S(6)} %min.11.refs_2_, bf16[64,16,1536]{2,1,0:T(8,128)(2,1)S(1)} %get-tuple-element.310.refs_3_), custom_call_target="tpu_custom_call" | custom-call | tf_op jit(solution)/shard_map/cond/branch_1_fun/while/body/pallas_call | solution.py:81
  103.2 0.0 copy-done.4
  103.2 0.9 collective-permute-start.10
  104.1 1.2 collective-permute-start.9
  105.3 24.7 %collective-permute-done.10 = bf16[32,16,1024]{2,1,0:T(8,128)(2,1)S(1)} collective-permute-done((bf16[32,16,1024]{2,1,0:T(8,128)(2,1)}, bf16[32,16,1024]{2,1,0:T(8,128)(2,1)S(1)}, u32[]{:S(2)}, u32[]{:S(2)}) %collective-permute-start.10) | collective-permute-done | bytes 1048608 | tf_op jit(solution)/shard_map/cond/branch_1_fun/while/body/ppermute | solution.py:147
  130.0 1.1 collective-permute-done.9
  131.1 0.0 all-gather.9.cloned.1.call-update
  131.1 1.5 collective-permute-start.11
  132.6 0.7 collective-permute-start.12
  133.3 1.3 collective-permute-start.15
  134.6 37.6 %collective-permute-done.11 = bf16[32,16,1024]{2,1,0:T(8,128)(2,1)S(1)} collective-permute-done((bf16[32,16,1024]{2,1,0:T(8,128)(2,1)}, bf16[32,16,1024]{2,1,0:T(8,128)(2,1)S(1)}, u32[]{:S(2)}, u32[]{:S(2)}) %collective-permute-start.11) | collective-permute-done | bytes 1048608 | tf_op jit(solution)/shard_map/cond/branch_1_fun/while/body/ppermute | solution.py:149
  172.3 0.0 collective-permute-done.12
  172.3 4.2 %collective-permute-start.13 = (bf16[32,16,1024]{2,1,0:T(8,128)(2,1)S(1)}, bf16[32,16,1024]{2,1,0:T(8,128)(2,1)}, u32[]{:S(2)}, u32[]{:S(2)}) collective-permute-start(bf16[32,16,1024]{2,1,0:T(8,128)(2,1)S(1)} %collective-permute-done.11), channel_id=1, source_target_pairs={{0,16},{1,49},{2,18},{3,51},{4,20},{5,53},{6,22},{7,55},{8,24},{9,... | collective-permute-start | bytes 3145736 | tf_op jit(solution)/shard_map/cond/branch_1_fun/while/body/ppermute | solution.py:162
  176.5 0.0 collective-permute-done.15
  176.5 0.1 collective-permute-start.16
  176.5 3.2 %collective-permute-start.17 = (bf16[32,16,1024]{2,1,0:T(8,128)(2,1)S(1)}, bf16[32,16,1024]{2,1,0:T(8,128)(2,1)}, u32[]{:S(2)}, u32[]{:S(2)}) collective-permute-start(bf16[32,16,1024]{2,1,0:T(8,128)(2,1)S(1)} %collective-permute-done.11), channel_id=1, source_target_pairs={{0,48},{1,17},{2,50},{3,19},{4,52},{5,21},{6,54},{7,23},{8,56},{9,... | collective-permute-start | bytes 3145736 | tf_op jit(solution)/shard_map/cond/branch_1_fun/while/body/ppermute | solution.py:163
  179.7 16.1 %collective-permute-done.13 = bf16[32,16,1024]{2,1,0:T(8,128)(2,1)} collective-permute-done((bf16[32,16,1024]{2,1,0:T(8,128)(2,1)S(1)}, bf16[32,16,1024]{2,1,0:T(8,128)(2,1)}, u32[]{:S(2)}, u32[]{:S(2)}) %collective-permute-start.13) | collective-permute-done | bytes 1048608 | tf_op jit(solution)/shard_map/cond/branch_1_fun/while/body/ppermute | solution.py:162
  195.9 2.6 %collective-permute-start.14 = (bf16[32,16,1024]{2,1,0:T(8,128)(2,1)}, bf16[32,16,1024]{2,1,0:T(8,128)(2,1)}, u32[]{:S(2)}, u32[]{:S(2)}) collective-permute-start(bf16[32,16,1024]{2,1,0:T(8,128)(2,1)} %collective-permute-done.13), channel_id=1, source_target_pairs={{0,16},{1,49},{2,18},{3,51},{4,20},{5,53},{6,22},{7,55},{8,24},{9,... | collective-permute-start | bytes 3145736 | tf_op jit(solution)/shard_map/cond/branch_1_fun/while/body/ppermute | solution.py:164
  198.4 0.1 concatenate.7.refs_0_
  198.5 13.6 %collective-permute-done.16 = bf16[32,16,1024]{2,1,0:T(8,128)(2,1)} collective-permute-done((bf16[32,16,1024]{2,1,0:T(8,128)(2,1)}, bf16[32,16,1024]{2,1,0:T(8,128)(2,1)}, u32[]{:S(2)}, u32[]{:S(2)}) %collective-permute-start.16) | collective-permute-done | bytes 1048608 | tf_op jit(solution)/shard_map/cond/branch_1_fun/while/body/ppermute | solution.py:164
  212.1 0.0 collective-permute-done.17
  212.1 0.0 all-gather.9.cloned.1.call-done
  212.1 0.0 copy-start
  212.1 2.2 copy-done
  214.3 0.0 copy-start.1
  214.3 7.2 %body.16.refs_3_ = f32[512,1024]{1,0:T(8,128)S(1)} custom-call(s32[7]{0:T(128)S(1)} %concatenate.7.refs_0_, bf16[8,512,512]{2,1,0:T(8,128)(2,1)S(1)} %bitcast.79, bf16[512,1024]{1,0:T(8,128)(2,1)S(1)} %bitcast.81, bf16[512,1024]{1,0:T(8,128)(2,1)} %bitcast.73.refs_3_, bf16[512,1024]{1,0:T(8,128)(2,1)S(1)} %bitcast.83, bf16[512,1024]{1,0:T(8,128)(2,1)} %bitcast.75.refs_5_, ...), custom_call_target="tpu_custom_call" | custom-call | flops 3758096384 | bytes 13107200 | tf_op jit(solution)/shard_map/cond/branch_1_fun/while/body/pallas_call | solution.py:128
  221.6 1.8 collective-permute-done.14
  223.4 0.0 copy-done.1
  223.4 0.0 copy-start.5
  223.4 3.7 %body.17 = f32[512,1024]{1,0:T(8,128)} custom-call(s32[1]{0:T(128)} %bitcast.61.refs_0_, bf16[8,512,512]{2,1,0:T(8,128)(2,1)S(1)} %bitcast.80, bf16[512,1024]{1,0:T(8,128)(2,1)} %bitcast.64.refs_2_, f32[512,1024]{1,0:T(8,128)S(1)} %body.16.refs_3_), custom_call_target="tpu_custom_call" | custom-call | flops 536870912 | bytes 3670016 | tf_op jit(solution)/shard_map/cond/branch_1_fun/while/body/pallas_call | solution.py:128
  227.1 0.0 copy-done.5
  227.1 1.8 fusion
  228.9 0.0 copy-start.6
  228.9 1.0 copy-done.6
  (6 shorter events, 0.1 us)
Async XLA Ops:
  9.7 12.2 %copy-start.7 = (s32[1,64,2]{1,2,0:T(2,128)S(1)}, s32[1,64,2]{1,2,0:T(2,128)}, u32[]{:S(2)}) copy-start(s32[1,64,2]{1,2,0:T(2,128)} %param.9) | copy-start | bytes 1540
  9.7 85.5 %all-to-all-start = ((bf16[64,16,1536]{2,1,0:T(8,128)(2,1)}), bf16[64,16,1536]{2,1,0:T(8,128)(2,1)S(1)}, u32[]{:S(2)}, u32[]{:S(2)}) async-start(bf16[64,16,1536]{2,1,0:T(8,128)(2,1)} %shard_map.39), calls=%async_computation | async-start | bytes 6291456 | tf_op jit(solution)/shard_map/all_to_all | solution.py:193
  21.9 4.4 %collective-permute-start.18 = (s32[1,64,2]{1,2,0:T(2,128)S(1)}, s32[1,64,2]{1,2,0:T(2,128)S(1)}, u32[]{:S(2)}, u32[]{:S(2)}) collective-permute-start(s32[1,64,2]{1,2,0:T(2,128)S(1)} %copy-done.7), channel_id=1, source_target_pairs={{0,64},{64,128},{128,192},{192,0},{1,65},{65,129},{129,193},{193,1... | collective-permute-start | bytes 1544 | tf_op jit(solution)/shard_map/ppermute | solution.py:187
  22.5 4.8 %collective-permute-start.20 = (s32[1,64,2]{1,2,0:T(2,128)S(1)}, s32[1,64,2]{1,2,0:T(2,128)S(1)}, u32[]{:S(2)}, u32[]{:S(2)}) collective-permute-start(s32[1,64,2]{1,2,0:T(2,128)S(1)} %copy-done.7), channel_id=1, source_target_pairs={{0,192},{64,0},{128,64},{192,128},{1,193},{65,1},{129,65},{193,129... | collective-permute-start | bytes 1544 | tf_op jit(solution)/shard_map/ppermute | solution.py:187
  24.0 5.1 %collective-permute-start.19 = (s32[1,64,2]{1,2,0:T(2,128)S(1)}, s32[1,64,2]{1,2,0:T(2,128)S(1)}, u32[]{:S(2)}, u32[]{:S(2)}) collective-permute-start(s32[1,64,2]{1,2,0:T(2,128)S(1)} %copy-done.7), channel_id=1, source_target_pairs={{0,128},{64,192},{128,0},{192,64},{1,129},{65,193},{129,1},{193,65... | collective-permute-start | bytes 1544 | tf_op jit(solution)/shard_map/ppermute | solution.py:187
  96.9 6.3 %copy-start.4 = (bf16[64,16,1536]{2,1,0:T(8,128)(2,1)}, bf16[64,16,1536]{2,1,0:T(8,128)(2,1)S(1)}, u32[]{:S(2)}) copy-start(bf16[64,16,1536]{2,1,0:T(8,128)(2,1)S(1)} %get-tuple-element.310.refs_3_) | copy-start | bytes 9437188 | tf_op jit(solution)/shard_map/cond/branch_1_fun/while
  96.9 115.3 %all-gather.9.cloned.1.call-start = ((), (), s32[]{:S(2)}) async-start(), calls=%async_computation.2 | async-start | bytes 4718592 | tf_op jit(solution)/shard_map/cond/branch_1_fun/while/body/all_gather | solution.py:153
  103.2 26.8 %collective-permute-start.10 = (bf16[32,16,1024]{2,1,0:T(8,128)(2,1)}, bf16[32,16,1024]{2,1,0:T(8,128)(2,1)S(1)}, u32[]{:S(2)}, u32[]{:S(2)}) collective-permute-start(bf16[32,16,1024]{2,1,0:T(8,128)(2,1)} %get-tuple-element.259), channel_id=1, source_target_pairs={{0,192},{64,0},{128,64},{192,128},{1,193},{65,1},{129,65},{193,129... | collective-permute-start | bytes 3145736 | tf_op jit(solution)/shard_map/cond/branch_1_fun/while/body/ppermute | solution.py:147
  104.1 27.0 %collective-permute-start.9 = (bf16[32,16,1024]{2,1,0:T(8,128)(2,1)}, bf16[32,16,1024]{2,1,0:T(8,128)(2,1)}, u32[]{:S(2)}, u32[]{:S(2)}) collective-permute-start(bf16[32,16,1024]{2,1,0:T(8,128)(2,1)} %get-tuple-element.259), channel_id=1, source_target_pairs={{0,4},{1,13},{2,6},{3,15},{4,8},{5,1},{6,10},{7,3},{8,12},{9,5},{1... | collective-permute-start | bytes 3145736 | tf_op jit(solution)/shard_map/cond/branch_1_fun/while/body/ppermute | solution.py:146
  131.1 41.2 %collective-permute-start.11 = (bf16[32,16,1024]{2,1,0:T(8,128)(2,1)}, bf16[32,16,1024]{2,1,0:T(8,128)(2,1)S(1)}, u32[]{:S(2)}, u32[]{:S(2)}) collective-permute-start(bf16[32,16,1024]{2,1,0:T(8,128)(2,1)} %collective-permute-done.9), channel_id=1, source_target_pairs={{0,196},{1,205},{2,198},{3,207},{4,200},{5,193},{6,202},{7,195},{8... | collective-permute-start | bytes 3145736 | tf_op jit(solution)/shard_map/cond/branch_1_fun/while/body/ppermute | solution.py:149
  132.6 39.7 %collective-permute-start.12 = (bf16[32,16,1024]{2,1,0:T(8,128)(2,1)S(1)}, bf16[32,16,1024]{2,1,0:T(8,128)(2,1)S(1)}, u32[]{:S(2)}, u32[]{:S(2)}) collective-permute-start(bf16[32,16,1024]{2,1,0:T(8,128)(2,1)S(1)} %collective-permute-done.10), channel_id=1, source_target_pairs={{0,48},{1,17},{2,50},{3,19},{4,52},{5,21},{6,54},{7,23},{8,56},{9,... | collective-permute-start | bytes 3145736 | tf_op jit(solution)/shard_map/cond/branch_1_fun/while/body/ppermute | solution.py:163
  133.3 43.1 %collective-permute-start.15 = (bf16[32,16,1024]{2,1,0:T(8,128)(2,1)S(1)}, bf16[32,16,1024]{2,1,0:T(8,128)(2,1)}, u32[]{:S(2)}, u32[]{:S(2)}) collective-permute-start(bf16[32,16,1024]{2,1,0:T(8,128)(2,1)S(1)} %collective-permute-done.10), channel_id=1, source_target_pairs={{0,16},{1,49},{2,18},{3,51},{4,20},{5,53},{6,22},{7,55},{8,24},{9,... | collective-permute-start | bytes 3145736 | tf_op jit(solution)/shard_map/cond/branch_1_fun/while/body/ppermute | solution.py:162
  172.3 23.6 %collective-permute-start.13 = (bf16[32,16,1024]{2,1,0:T(8,128)(2,1)S(1)}, bf16[32,16,1024]{2,1,0:T(8,128)(2,1)}, u32[]{:S(2)}, u32[]{:S(2)}) collective-permute-start(bf16[32,16,1024]{2,1,0:T(8,128)(2,1)S(1)} %collective-permute-done.11), channel_id=1, source_target_pairs={{0,16},{1,49},{2,18},{3,51},{4,20},{5,53},{6,22},{7,55},{8,24},{9,... | collective-permute-start | bytes 3145736 | tf_op jit(solution)/shard_map/cond/branch_1_fun/while/body/ppermute | solution.py:162
  176.5 35.7 %collective-permute-start.16 = (bf16[32,16,1024]{2,1,0:T(8,128)(2,1)}, bf16[32,16,1024]{2,1,0:T(8,128)(2,1)}, u32[]{:S(2)}, u32[]{:S(2)}) collective-permute-start(bf16[32,16,1024]{2,1,0:T(8,128)(2,1)} %collective-permute-done.15), channel_id=1, source_target_pairs={{0,16},{1,49},{2,18},{3,51},{4,20},{5,53},{6,22},{7,55},{8,24},{9,... | collective-permute-start | bytes 3145736 | tf_op jit(solution)/shard_map/cond/branch_1_fun/while/body/ppermute | solution.py:164
  176.5 35.6 %collective-permute-start.17 = (bf16[32,16,1024]{2,1,0:T(8,128)(2,1)S(1)}, bf16[32,16,1024]{2,1,0:T(8,128)(2,1)}, u32[]{:S(2)}, u32[]{:S(2)}) collective-permute-start(bf16[32,16,1024]{2,1,0:T(8,128)(2,1)S(1)} %collective-permute-done.11), channel_id=1, source_target_pairs={{0,48},{1,17},{2,50},{3,19},{4,52},{5,21},{6,54},{7,23},{8,56},{9,... | collective-permute-start | bytes 3145736 | tf_op jit(solution)/shard_map/cond/branch_1_fun/while/body/ppermute | solution.py:163
  195.9 27.5 %collective-permute-start.14 = (bf16[32,16,1024]{2,1,0:T(8,128)(2,1)}, bf16[32,16,1024]{2,1,0:T(8,128)(2,1)}, u32[]{:S(2)}, u32[]{:S(2)}) collective-permute-start(bf16[32,16,1024]{2,1,0:T(8,128)(2,1)} %collective-permute-done.13), channel_id=1, source_target_pairs={{0,16},{1,49},{2,18},{3,51},{4,20},{5,53},{6,22},{7,55},{8,24},{9,... | collective-permute-start | bytes 3145736 | tf_op jit(solution)/shard_map/cond/branch_1_fun/while/body/ppermute | solution.py:164
  212.1 2.2 copy-start
  214.3 9.0 %copy-start.1 = (bf16[256,16,512]{2,1,0:T(8,128)(2,1)S(1)}, bf16[256,16,512]{2,1,0:T(8,128)(2,1)}, u32[]{:S(2)}) copy-start(bf16[256,16,512]{2,1,0:T(8,128)(2,1)} %all-gather.9.cloned.1.call-done) | copy-start | bytes 12582916 | tf_op jit(solution)/shard_map/cond/branch_1_fun/while
  223.4 3.7 %copy-start.5 = (bf16[64,16,1536]{2,1,0:T(8,128)(2,1)S(1)}, bf16[64,16,1536]{2,1,0:T(8,128)(2,1)}, u32[]{:S(2)}) copy-start(bf16[64,16,1536]{2,1,0:T(8,128)(2,1)} %copy-done.4) | copy-start | bytes 9437188 | tf_op jit(solution)/shard_map/cond/branch_1_fun/while
  228.9 1.0 copy-start.6
Sparse Core Ops, SparseCore 0:
  131.2 64.7 all-gather.8
